TPU v7x, 32 devices: a whole 2x2x4 slice. The times are simulated.
32 devices in a mesh: section: 4 (over y, x), band: 4 (over z), members: 2 (over core).
Axes of the slice: x: 2, y: 2, z: 4, core: 2. Of those that a mesh axis runs over, the one named last changes fastest.
Arguments:
- fields: bfloat16 [8, 16, 576, 128], P(('members', 'section'), 'band'), parts along dimension 0, may hold values from -6 to 6
- lat_taps: bfloat16 [2, 9, 128], replicated, may hold values from -1.5 to 1.5
- lon_taps: bfloat16 [2, 9, 128], replicated, may hold values from -1.5 to 1.5
- gains: float32 [2, 128], replicated, may hold values from 0.1 to 1.9
- w_in: bfloat16 [2, 128, 256], replicated, may hold values from -0.5 to 0.5
- w_out: bfloat16 [2, 256, 128], replicated, may hold values from -0.375 to 0.375
Outputs:
- final_states: bfloat16 [8, 16, 576, 128], P(('members', 'section'), 'band'), parts along dimension 0
There are 2 independent parts, one for each index of `members`. A program takes and returns all parts, laid end to end along the dimension named above; an argument that names none is the same for every part. Nothing has to cross between parts.
All inputs are finite; a program needn't handle non-finite values.
Results may differ from a plain program's by a relative error of at most 0.0063.
Values may be sent and summed in bfloat16 or wider, within the bound.
No kernel may reach another device: no remote copies, remote signals or barrier semaphores. Data moves between devices by JAX's collectives and lax.ppermute only.
A program may use at most 64 MiB of HBM per device.

v0:
```python
import functools

import jax
import jax.numpy as jnp
from jax import lax
from jax.experimental import pallas as pl
from jax.experimental.pallas import tpu as pltpu
from jax.sharding import PartitionSpec as P

DLON = 3
LAYERS = 2
TAPS = 9
REACH = TAPS // 2
PAD = 16
TILE = 32


def gelu(x):
    return 0.5 * x * (1.0 + lax.erf(x * 0.7071067811865476))


def copy_kernel(lo, state, *refs):
    out = refs[-1]
    out[...] = state[:, lo : lo + out.shape[1]]


def later_columns(state, lo, hi, after):
    rows, _, channels = state.shape
    return pl.pallas_call(
        functools.partial(copy_kernel, lo),
        out_shape=jax.ShapeDtypeStruct((rows, hi - lo, channels), state.dtype),
        in_specs=[pl.BlockSpec(memory_space=pltpu.VMEM)] * (1 + len(after)),
        out_specs=pl.BlockSpec(memory_space=pltpu.VMEM),
        compiler_params=pltpu.CompilerParams(vmem_limit_bytes=16 * 2**20),
        cost_estimate=pl.CostEstimate(flops=2 * 10**9, bytes_accessed=4 * rows * (hi - lo) * channels, transcendentals=0),
    )(state, *after)


def chunk_kernel(layer, first, last, offset, width, prev_end, place, *refs):
    refs = list(refs)
    lat_w, lon_w, gain, w_in, w_out, own, odd_swap, even_swap = refs[:8]
    refs = refs[8:]
    if not first:
        prev_own, prev_mix = refs[:2]
        refs = refs[2:]
    if last and not first:
        first_own, first_mix = refs[:2]
        refs = refs[2:]
    if place is not None and not first:
        refs.pop(0)
    out = refs.pop(0)
    if not last:
        tail = refs.pop(0)
    if first and not last:
        head = refs.pop(0)
    mix, state = refs[:2]
    whole = out
    if place is not None:
        out, sems = refs[2:]
    rows = own.shape[0]
    channels = own.shape[2]
    start = 0 if first else 2 * PAD

    if not first:
        mix[:, : 2 * PAD] = prev_mix[...].astype(jnp.float32)
        state[:, : 2 * PAD] = prev_own[:, prev_end - 2 * PAD : prev_end]
    if last and not first:
        mix[:, start + width :] = first_mix[...].astype(jnp.float32)
        state[:, start + width :] = first_own[:, : 2 * PAD]

    band = lax.axis_index("band")
    is_odd = lax.rem(band, 2) == 1
    lat_rows = lat_w[...].astype(jnp.float32)
    lat_tap = [jnp.broadcast_to(lat_rows[k, layer : layer + 1], (PAD, channels)) for k in range(TAPS)]

    def mix_tile(t, carry):
        at = pl.multiple_of(offset + t * PAD, PAD)
        to = pl.multiple_of(start + t * PAD, PAD)
        evens = [even_swap[r, pl.ds(at, PAD)] for r in range(REACH)]
        odds = [odd_swap[r, pl.ds(at, PAD)] for r in range(REACH)]
        above = [jnp.where(is_odd, e, o) for e, o in zip(evens, odds)]
        below = [jnp.where(is_odd, o, e) for e, o in zip(evens, odds)]
        mine = [own[r, pl.ds(at, PAD)] for r in range(rows)]
        strip = [s.astype(jnp.float32) for s in above + mine + below]
        for r in range(rows):
            total = strip[r] * lat_tap[0]
            for k in range(1, TAPS):
                total = total + strip[r + k] * lat_tap[k]
            mix[r, pl.ds(to, PAD)] = total.astype(jnp.bfloat16).astype(jnp.float32)
            state[r, pl.ds(to, PAD)] = mine[r]
        return carry

    lax.fori_loop(0, width // PAD, mix_tile, 0, unroll=2)

    if not last:
        tail[...] = mix[:, start + width - 2 * PAD : start + width].astype(jnp.bfloat16)
    if first and not last:
        head[...] = mix[:, : 2 * PAD].astype(jnp.bfloat16)
    if first and last:
        mix[:, width:] = mix[:, : 2 * PAD]
        state[:, width:] = state[:, : 2 * PAD]

    lon_rows = lon_w[...].astype(jnp.float32)
    lon_tap = [lon_rows[k, layer : layer + 1] for k in range(TAPS)]
    scale = gain[layer : layer + 1]
    made, total = out.shape[1], whole.shape[1]

    def rest(at, tile):
        parts = []
        for r in range(rows):
            lon = mix[r, pl.ds(at + PAD - DLON * REACH, tile)] * lon_tap[0]
            for k in range(1, TAPS):
                lon = lon + mix[r, pl.ds(at + PAD + DLON * (k - REACH), tile)] * lon_tap[k]
            parts.append(lon)
        lon = jnp.concatenate(parts, axis=0)
        mean = jnp.mean(lon, axis=-1, keepdims=True)
        centred = lon - mean
        var = jnp.mean(centred * centred, axis=-1, keepdims=True)
        normed = (centred * lax.rsqrt(var + 1e-06) * scale).astype(jnp.bfloat16)
        hidden = jnp.dot(normed, w_in[layer], preferred_element_type=jnp.float32)
        hidden = gelu(hidden).astype(jnp.bfloat16)
        delta = jnp.dot(hidden, w_out[layer], preferred_element_type=jnp.float32)
        for r in range(rows):
            new = state[r, pl.ds(at + PAD, tile)].astype(jnp.float32) + delta[r * tile : (r + 1) * tile]
            out[r, pl.ds(at, tile)] = new.astype(jnp.bfloat16)

    copies = []
    for at, tile in tiles(made, total, place):
        rest(at, tile)
        if place is not None:
            to = (place + at) % total
            copies.append(
                pltpu.make_async_copy(out.at[:, at : at + tile], whole.at[:, to : to + tile], sems.at[len(copies)])
            )
            copies[-1].start()
    for copy in copies:
        copy.wait()


def tiles(made, total, place):
    edges = set(range(0, made, TILE)) | {made}
    if place is not None and place + made > total:
        edges = set(range(0, total - place, TILE)) | set(range(total - place, made, TILE)) | {made}
    edges = sorted(edges)
    return [(lo, hi - lo) for lo, hi in zip(edges[:-1], edges[1:])]


def layer_chunk(layer, weights, chunk, offset, width, prev, first_chunk, first, last, place=None, whole=None):
    own = chunk[0]
    rows, _, channels = own.shape
    prev_end = None if first else prev[1]
    made = width + (0 if first else PAD) + (0 if last else -PAD) + (PAD if last else 0) - (PAD if first else 0)
    window = made + 2 * PAD
    args = list(weights) + list(chunk)
    if not first:
        args += [prev[0], prev[2]]
    if last and not first:
        args += list(first_chunk)
    specs = [pl.BlockSpec(memory_space=pltpu.VMEM)] * len(args)
    strip = jax.ShapeDtypeStruct((rows, 2 * PAD, channels), jnp.bfloat16)
    outs = [jax.ShapeDtypeStruct((rows, made, channels), jnp.bfloat16)]
    out_specs = [pl.BlockSpec(memory_space=pltpu.VMEM)]
    scratch = [
        pltpu.VMEM((rows, window, channels), jnp.float32),
        pltpu.VMEM((rows, window, channels), jnp.bfloat16),
    ]
    aliases = {}
    if place is not None:
        lons = whole if first else whole.shape[1]
        scratch += [pltpu.VMEM(outs[0].shape, jnp.bfloat16), pltpu.SemaphoreType.DMA((len(tiles(made, lons, place)),))]
        outs = [jax.ShapeDtypeStruct((rows, lons, channels), jnp.bfloat16)]
        out_specs = [pl.BlockSpec(memory_space=pltpu.HBM)]
        if not first:
            aliases = {len(args): 0}
            args.append(whole)
            specs += out_specs
    if not last:
        outs.append(strip)
    if first and not last:
        outs.append(strip)
    out_specs += [pl.BlockSpec(memory_space=pltpu.VMEM)] * (len(outs) - 1)
    cells = rows * made
    hidden = weights[3].shape[2]
    return pl.pallas_call(
        functools.partial(chunk_kernel, layer, first, last, offset, width, prev_end, place),
        out_shape=outs,
        in_specs=specs,
        out_specs=out_specs,
        scratch_shapes=scratch,
        input_output_aliases=aliases,
        compiler_params=pltpu.CompilerParams(vmem_limit_bytes=24 * 2**20),
        cost_estimate=pl.CostEstimate(
            flops=50 * cells * channels * hidden, bytes_accessed=8 * cells * channels, transcendentals=cells * hidden
        ),
    )(*args)


def splits(total):
    first = PAD * ((total // PAD + 2) // 2)
    return [(0, first), (first, total)]


def swaps(bands, start):
    return [pair for b in range(start, bands - 1, 2) for pair in ((b, b + 1), (b + 1, b))]


def member_step(state, weights, bands):
    rows, lons, _ = state.shape
    assert rows == REACH
    even_pairs, odd_pairs = swaps(bands, 0), swaps(bands, 1)
    ranges = splits(lons)
    chunks = [state[:, : ranges[0][1]]]
    for lo, hi in ranges[1:]:
        chunks.append(later_columns(state, lo, hi, weights))
    whole, place = lons, LAYERS * PAD
    for layer in range(LAYERS):
        halos = []
        for own in chunks:
            odd_swap = lax.ppermute(own, "band", odd_pairs)
            even_swap = lax.ppermute(own, "band", even_pairs)
            halos.append((odd_swap, even_swap))
        final = layer == LAYERS - 1
        pieces = [(c, 0, own.shape[1]) for c, own in enumerate(chunks)]
        if layer == 0:
            c, _, width = pieces.pop()
            cut = 2 * PAD * (width * 3 // (8 * PAD))
            pieces += [(c, 0, cut), (c, cut, width - cut)]
        made, prev, first_chunk = [], None, None
        for p, (c, offset, width) in enumerate(pieces):
            own = chunks[c]
            first, last = p == 0, p == len(pieces) - 1
            where = (place, whole) if final else ()
            got = layer_chunk(
                layer, weights, (own,) + halos[c], offset, width, prev, first_chunk, first, last, *where
            )
            made.append(got[0])
            if final:
                whole = got[0]
                place += width - (2 * PAD if first else 0)
            if not last:
                prev = (own, offset + width, got[1])
            if first and not last:
                first_chunk = (own, got[2])
        chunks = made
    return whole


def solution(mesh):
    bands = mesh.shape["band"]

    def shards(fields, lat_taps, lon_taps, gains, w_in, w_out):
        weights = (lat_taps.transpose(1, 0, 2), lon_taps.transpose(1, 0, 2), gains, w_in, w_out)
        return jnp.concatenate([member_step(fields[m], weights, bands)[None] for m in range(fields.shape[0])])

    return jax.shard_map(
        shards,
        mesh=mesh,
        in_specs=(P(("members", "section"), "band", None, None), P(), P(), P(), P(), P()),
        out_specs=P(("members", "section"), "band", None, None),
        check_vma=False,
    )
```

profile of v0, /device:TPU:0, one launch (start us, length us, event | category | flops | bytes accessed | tf_op | source)
XLA Modules:
  0.0 35.4 jit_solution(10327797257997692997)
XLA Ops:
  0.0 1.1 %slice.4.refs_5_.refs_8_.refs_10_ = bf16[4,304,128]{2,1,0:T(8,128)(2,1)S(1)} slice(bf16[4,576,128]{2,1,0:T(8,128)(2,1)} %bitcast.4), slice={[0:4], [0:304], [0:128]} | slice | bytes 622592 | tf_op jit(solution)/shard_map/slice | solution.py:212
  1.1 3.1 %collective-permute-start.3 = (bf16[4,304,128]{2,1,0:T(8,128)(2,1)S(1)}, bf16[4,304,128]{2,1,0:T(8,128)(2,1)S(1)}, u32[]{:S(2)}, u32[]{:S(2)}) collective-permute-start(bf16[4,304,128]{2,1,0:T(8,128)(2,1)S(1)} %slice.4.refs_5_.refs_8_.refs_10_), channel_id=1, source_target_pairs={{0,2},{2,0},{4,6},{6,4},{1,3},{3,1},{5,7},{7,5},{8,10},{10,8},{12,... | collective-permute-start | bytes 933896 | tf_op jit(solution)/shard_map/ppermute | solution.py:220
  4.2 0.7 %collective-permute-start.2 = (bf16[4,304,128]{2,1,0:T(8,128)(2,1)S(1)}, bf16[4,304,128]{2,1,0:T(8,128)(2,1)S(1)}, u32[]{:S(2)}, u32[]{:S(2)}) collective-permute-start(bf16[4,304,128]{2,1,0:T(8,128)(2,1)S(1)} %slice.4.refs_5_.refs_8_.refs_10_), channel_id=1, source_target_pairs={{2,4},{4,2},{3,5},{5,3},{10,12},{12,10},{11,13},{13,11},{18,20},{2... | collective-permute-start | bytes 933896 | tf_op jit(solution)/shard_map/ppermute | solution.py:219
  4.8 0.0 copy-start.7
  4.9 0.6 %copy-done.7 = f32[2,128]{1,0:T(2,128)S(1)} copy-done((f32[2,128]{1,0:T(2,128)S(1)}, f32[2,128]{1,0:T(2,128)}, u32[]{:S(2)}) %copy-start.7) | copy-done | bytes 1048
  5.5 0.9 %copy-done.1 = bf16[2,128,256]{2,1,0:T(8,128)(2,1)S(1)} copy-done((bf16[2,128,256]{2,1,0:T(8,128)(2,1)S(1)}, bf16[2,128,256]{2,1,0:T(8,128)(2,1)}, u32[]{:S(2)}) %copy-start.1) | copy-done | bytes 131096
  6.4 0.9 %copy-done.3 = bf16[2,256,128]{2,1,0:T(8,128)(2,1)S(1)} copy-done((bf16[2,256,128]{2,1,0:T(8,128)(2,1)S(1)}, bf16[2,256,128]{2,1,0:T(8,128)(2,1)}, u32[]{:S(2)}) %copy-start.3) | copy-done | bytes 131096
  7.3 0.0 copy-start.4
  7.4 4.4 %collective-permute-start.1 = (bf16[4,272,128]{2,1,0:T(8,128)(2,1)S(1)}, bf16[4,272,128]{2,1,0:T(8,128)(2,1)S(1)}, u32[]{:S(2)}, u32[]{:S(2)}) collective-permute-start(bf16[4,272,128]{2,1,0:T(8,128)(2,1)S(1)} %shard_map.64.refs_5_.refs_8_), channel_id=1, source_target_pairs={{0,2},{2,0},{4,6},{6,4},{1,3},{3,1},{5,7},{7,5},{8,10},{10,8},{12,... | collective-permute-start | bytes 835592 | tf_op jit(solution)/shard_map/ppermute | solution.py:220
  11.8 0.7 %collective-permute-start = (bf16[4,272,128]{2,1,0:T(8,128)(2,1)S(1)}, bf16[4,272,128]{2,1,0:T(8,128)(2,1)S(1)}, u32[]{:S(2)}, u32[]{:S(2)}) collective-permute-start(bf16[4,272,128]{2,1,0:T(8,128)(2,1)S(1)} %shard_map.64.refs_5_.refs_8_), channel_id=1, source_target_pairs={{2,4},{4,2},{3,5},{5,3},{10,12},{12,10},{11,13},{13,11},{18,20},{2... | collective-permute-start | bytes 835592 | tf_op jit(solution)/shard_map/ppermute | solution.py:219
  12.5 0.0 collective-permute-done.3.refs_7_
  12.5 0.0 collective-permute-done.2.refs_6_
  12.5 1.6 %shard_map.65 = (bf16[4,272,128]{2,1,0:T(8,128)(2,1)S(1)}, bf16[4,32,128]{2,1,0:T(8,128)(2,1)S(1)}, bf16[4,32,128]{2,1,0:T(8,128)(2,1)S(1)}) custom-call(bf16[9,2,128]{2,1,0:T(2,128)(2,1)S(1)} %bitcast.7, bf16[9,2,128]{2,1,0:T(2,128)(2,1)S(1)} %bitcast.14, f32[2,128]{1,0:T(2,128)S(1)} %copy-done.7, bf16[2,128,256]{2,1,0:T(8,128)(2,1)S(1)} %copy-done.2, ...), custom_call_target="tpu_custom_call" | custom-call | flops 1782579200 | bytes 1114112 | tf_op jit(solution)/shard_map/pallas_call | solution.py:184
  14.1 4.5 %collective-permute-start.9 = (bf16[4,272,128]{2,1,0:T(8,128)(2,1)S(1)}, bf16[4,272,128]{2,1,0:T(8,128)(2,1)S(1)}, u32[]{:S(2)}, u32[]{:S(2)}) collective-permute-start(bf16[4,272,128]{2,1,0:T(8,128)(2,1)S(1)} %get-tuple-element.19.refs_5_.refs_8_.refs_10_), channel_id=1, source_target_pairs={{0,2},{2,0},{4,6},{6,4},{1,3},{3,1},{5,7},{7,5},{8,10},{10,8},{12,... | collective-permute-start | bytes 835592 | tf_op jit(solution)/shard_map/ppermute | solution.py:220
  18.7 0.7 %collective-permute-start.8 = (bf16[4,272,128]{2,1,0:T(8,128)(2,1)S(1)}, bf16[4,272,128]{2,1,0:T(8,128)(2,1)S(1)}, u32[]{:S(2)}, u32[]{:S(2)}) collective-permute-start(bf16[4,272,128]{2,1,0:T(8,128)(2,1)S(1)} %get-tuple-element.19.refs_5_.refs_8_.refs_10_), channel_id=1, source_target_pairs={{2,4},{4,2},{3,5},{5,3},{10,12},{12,10},{11,13},{13,11},{18,20},{2... | collective-permute-start | bytes 835592 | tf_op jit(solution)/shard_map/ppermute | solution.py:219
  19.4 1.2 %shard_map.66 = (bf16[4,192,128]{2,1,0:T(8,128)(2,1)S(1)}, bf16[4,32,128]{2,1,0:T(8,128)(2,1)S(1)}) custom-call(bf16[9,2,128]{2,1,0:T(2,128)(2,1)S(1)} %bitcast.8, bf16[9,2,128]{2,1,0:T(2,128)(2,1)S(1)} %bitcast.15, f32[2,128]{1,0:T(2,128)S(1)} %copy-done.7, bf16[2,128,256]{2,1,0:T(8,128)(2,1)S(1)} %copy-done.2, bf16[2,256,128]{2,1,0:T(8,128)(2,1)S(1)} %copy-done.4, ...), custom_call_target="tpu_custom_call" | custom-call | flops 1258291200 | bytes 786432 | tf_op jit(solution)/shard_map/pallas_call | solution.py:184
  20.6 3.8 %collective-permute-start.7 = (bf16[4,192,128]{2,1,0:T(8,128)(2,1)S(1)}, bf16[4,192,128]{2,1,0:T(8,128)(2,1)S(1)}, u32[]{:S(2)}, u32[]{:S(2)}) collective-permute-start(bf16[4,192,128]{2,1,0:T(8,128)(2,1)S(1)} %get-tuple-element.18.refs_5_.refs_8_), channel_id=1, source_target_pairs={{0,2},{2,0},{4,6},{6,4},{1,3},{3,1},{5,7},{7,5},{8,10},{10,8},{12,... | collective-permute-start | bytes 589832 | tf_op jit(solution)/shard_map/ppermute | solution.py:220
  24.4 0.7 %collective-permute-start.6 = (bf16[4,192,128]{2,1,0:T(8,128)(2,1)S(1)}, bf16[4,192,128]{2,1,0:T(8,128)(2,1)S(1)}, u32[]{:S(2)}, u32[]{:S(2)}) collective-permute-start(bf16[4,192,128]{2,1,0:T(8,128)(2,1)S(1)} %get-tuple-element.18.refs_5_.refs_8_), channel_id=1, source_target_pairs={{2,4},{4,2},{3,5},{5,3},{10,12},{12,10},{11,13},{13,11},{18,20},{2... | collective-permute-start | bytes 589832 | tf_op jit(solution)/shard_map/ppermute | solution.py:219
  25.0 0.8 %shard_map.67.refs_5_ = bf16[4,112,128]{2,1,0:T(8,128)(2,1)S(1)} custom-call(bf16[9,2,128]{2,1,0:T(2,128)(2,1)S(1)} %bitcast.9, bf16[9,2,128]{2,1,0:T(2,128)(2,1)S(1)} %bitcast.16, f32[2,128]{1,0:T(2,128)S(1)} %copy-done.7, bf16[2,128,256]{2,1,0:T(8,128)(2,1)S(1)} %copy-done.2, bf16[2,256,128]{2,1,0:T(8,128)(2,1)S(1)} %copy-done.4, ...), custom_call_target="tpu_custom_call" | custom-call | flops 734003200 | bytes 458752 | tf_op jit(solution)/shard_map/pallas_call | solution.py:184
  25.8 3.2 %collective-permute-start.5 = (bf16[4,112,128]{2,1,0:T(8,128)(2,1)S(1)}, bf16[4,112,128]{2,1,0:T(8,128)(2,1)S(1)}, u32[]{:S(2)}, u32[]{:S(2)}) collective-permute-start(bf16[4,112,128]{2,1,0:T(8,128)(2,1)S(1)} %shard_map.67.refs_5_), channel_id=1, source_target_pairs={{0,2},{2,0},{4,6},{6,4},{1,3},{3,1},{5,7},{7,5},{8,10},{10,8},{12,... | collective-permute-start | bytes 344072 | tf_op jit(solution)/shard_map/ppermute | solution.py:220
  29.1 0.7 %collective-permute-start.4 = (bf16[4,112,128]{2,1,0:T(8,128)(2,1)S(1)}, bf16[4,112,128]{2,1,0:T(8,128)(2,1)S(1)}, u32[]{:S(2)}, u32[]{:S(2)}) collective-permute-start(bf16[4,112,128]{2,1,0:T(8,128)(2,1)S(1)} %shard_map.67.refs_5_), channel_id=1, source_target_pairs={{2,4},{4,2},{3,5},{5,3},{10,12},{12,10},{11,13},{13,11},{18,20},{2... | collective-permute-start | bytes 344072 | tf_op jit(solution)/shard_map/ppermute | solution.py:219
  29.7 2.2 %shard_map.68 = (bf16[4,576,128]{2,1,0:T(8,128)(2,1)}, bf16[4,32,128]{2,1,0:T(8,128)(2,1)S(1)}, bf16[4,32,128]{2,1,0:T(8,128)(2,1)S(1)}) custom-call(bf16[9,2,128]{2,1,0:T(2,128)(2,1)S(1)} %bitcast.10, bf16[9,2,128]{2,1,0:T(2,128)(2,1)S(1)} %bitcast.17, f32[2,128]{1,0:T(2,128)S(1)} %copy-done.7, bf16[2,128,256]{2,1,0:T(8,128)(2,1)S(1)} %copy-done.2, ...), custom_call_target="tpu_custom_call" | custom-call | flops 1572864000 | bytes 983040 | tf_op jit(solution)/shard_map/pallas_call | solution.py:184
  31.9 1.9 %shard_map.69 = (bf16[4,576,128]{2,1,0:T(8,128)(2,1)}, bf16[4,32,128]{2,1,0:T(8,128)(2,1)S(1)}) custom-call(bf16[9,2,128]{2,1,0:T(2,128)(2,1)S(1)} %bitcast.11, bf16[9,2,128]{2,1,0:T(2,128)(2,1)S(1)} %bitcast.18, f32[2,128]{1,0:T(2,128)S(1)} %copy-done.7, bf16[2,128,256]{2,1,0:T(8,128)(2,1)S(1)} %copy-done.2, ...), custom_call_target="tpu_custom_call", output_to_operand_aliasing={{0}: (10, {})} | custom-call | flops 1258291200 | bytes 786432 | tf_op jit(solution)/shard_map/pallas_call | solution.py:184
  33.8 1.6 %shard_map.70 = bf16[4,576,128]{2,1,0:T(8,128)(2,1)} custom-call(bf16[9,2,128]{2,1,0:T(2,128)(2,1)S(1)} %bitcast.12, bf16[9,2,128]{2,1,0:T(2,128)(2,1)S(1)} %bitcast.19, f32[2,128]{1,0:T(2,128)S(1)} %copy-done.7, bf16[2,128,256]{2,1,0:T(8,128)(2,1)S(1)} %copy-done.2, bf16[2,256,128]{2,1,0:T(8,128)(2,1)S(1)} %copy-done.4, ...), custom_call_target="tpu_custom_call", output_to_operand_aliasing={{}: (12, {})} | custom-call | flops 943718400 | bytes 589824 | tf_op jit(solution)/shard_map/pallas_call | solution.py:184
  (20 shorter events, 0.1 us)
Async XLA Ops:
  0.0 4.8 %copy-start = (bf16[1,4,576,128]{3,2,1,0:T(8,128)(2,1)S(1)}, bf16[1,4,576,128]{3,2,1,0:T(8,128)(2,1)}, u32[]{:S(2)}) copy-start(bf16[1,4,576,128]{3,2,1,0:T(8,128)(2,1)} %param.6) | copy-start | bytes 1769476
  0.0 4.9 %copy-start.5 = (bf16[2,9,128]{2,0,1:T(2,128)(2,1)S(1)}, bf16[2,9,128]{2,0,1:T(2,128)(2,1)}, u32[]{:S(2)}) copy-start(bf16[2,9,128]{2,0,1:T(2,128)(2,1)} %param.7) | copy-start | bytes 13828
  0.0 4.9 %copy-start.6 = (bf16[2,9,128]{2,0,1:T(2,128)(2,1)S(1)}, bf16[2,9,128]{2,0,1:T(2,128)(2,1)}, u32[]{:S(2)}) copy-start(bf16[2,9,128]{2,0,1:T(2,128)(2,1)} %param.8) | copy-start | bytes 13828
  1.1 11.4 %collective-permute-start.3 = (bf16[4,304,128]{2,1,0:T(8,128)(2,1)S(1)}, bf16[4,304,128]{2,1,0:T(8,128)(2,1)S(1)}, u32[]{:S(2)}, u32[]{:S(2)}) collective-permute-start(bf16[4,304,128]{2,1,0:T(8,128)(2,1)S(1)} %slice.4.refs_5_.refs_8_.refs_10_), channel_id=1, source_target_pairs={{0,2},{2,0},{4,6},{6,4},{1,3},{3,1},{5,7},{7,5},{8,10},{10,8},{12,... | collective-permute-start | bytes 933896 | tf_op jit(solution)/shard_map/ppermute | solution.py:220
  4.2 8.3 %collective-permute-start.2 = (bf16[4,304,128]{2,1,0:T(8,128)(2,1)S(1)}, bf16[4,304,128]{2,1,0:T(8,128)(2,1)S(1)}, u32[]{:S(2)}, u32[]{:S(2)}) collective-permute-start(bf16[4,304,128]{2,1,0:T(8,128)(2,1)S(1)} %slice.4.refs_5_.refs_8_.refs_10_), channel_id=1, source_target_pairs={{2,4},{4,2},{3,5},{5,3},{10,12},{12,10},{11,13},{13,11},{18,20},{2... | collective-permute-start | bytes 933896 | tf_op jit(solution)/shard_map/ppermute | solution.py:219
  4.8 0.7 %copy-start.7 = (f32[2,128]{1,0:T(2,128)S(1)}, f32[2,128]{1,0:T(2,128)}, u32[]{:S(2)}) copy-start(f32[2,128]{1,0:T(2,128)} %refs_2_.13) | copy-start | bytes 3076
  5.5 0.9 %copy-start.1 = (bf16[2,128,256]{2,1,0:T(8,128)(2,1)S(1)}, bf16[2,128,256]{2,1,0:T(8,128)(2,1)}, u32[]{:S(2)}) copy-start(bf16[2,128,256]{2,1,0:T(8,128)(2,1)} %refs_3_.13) | copy-start | bytes 393220
  6.4 0.9 %copy-start.3 = (bf16[2,256,128]{2,1,0:T(8,128)(2,1)S(1)}, bf16[2,256,128]{2,1,0:T(8,128)(2,1)}, u32[]{:S(2)}) copy-start(bf16[2,256,128]{2,1,0:T(8,128)(2,1)} %refs_4_.13) | copy-start | bytes 393220
  7.3 5.2 %copy-start.2 = (bf16[2,128,256]{2,1,0:T(8,128)(2,1)S(1)}, bf16[2,128,256]{2,1,0:T(8,128)(2,1)}, u32[]{:S(2)}) copy-start(bf16[2,128,256]{2,1,0:T(8,128)(2,1)} %refs_3_.13) | copy-start | bytes 393220
  7.3 12.0 %copy-start.4 = (bf16[2,256,128]{2,1,0:T(8,128)(2,1)S(1)}, bf16[2,256,128]{2,1,0:T(8,128)(2,1)}, u32[]{:S(2)}) copy-start(bf16[2,256,128]{2,1,0:T(8,128)(2,1)} %refs_4_.13) | copy-start | bytes 393220
  7.4 12.0 %collective-permute-start.1 = (bf16[4,272,128]{2,1,0:T(8,128)(2,1)S(1)}, bf16[4,272,128]{2,1,0:T(8,128)(2,1)S(1)}, u32[]{:S(2)}, u32[]{:S(2)}) collective-permute-start(bf16[4,272,128]{2,1,0:T(8,128)(2,1)S(1)} %shard_map.64.refs_5_.refs_8_), channel_id=1, source_target_pairs={{0,2},{2,0},{4,6},{6,4},{1,3},{3,1},{5,7},{7,5},{8,10},{10,8},{12,... | collective-permute-start | bytes 835592 | tf_op jit(solution)/shard_map/ppermute | solution.py:220
  11.8 7.6 %collective-permute-start = (bf16[4,272,128]{2,1,0:T(8,128)(2,1)S(1)}, bf16[4,272,128]{2,1,0:T(8,128)(2,1)S(1)}, u32[]{:S(2)}, u32[]{:S(2)}) collective-permute-start(bf16[4,272,128]{2,1,0:T(8,128)(2,1)S(1)} %shard_map.64.refs_5_.refs_8_), channel_id=1, source_target_pairs={{2,4},{4,2},{3,5},{5,3},{10,12},{12,10},{11,13},{13,11},{18,20},{2... | collective-permute-start | bytes 835592 | tf_op jit(solution)/shard_map/ppermute | solution.py:219
  14.1 14.9 %collective-permute-start.9 = (bf16[4,272,128]{2,1,0:T(8,128)(2,1)S(1)}, bf16[4,272,128]{2,1,0:T(8,128)(2,1)S(1)}, u32[]{:S(2)}, u32[]{:S(2)}) collective-permute-start(bf16[4,272,128]{2,1,0:T(8,128)(2,1)S(1)} %get-tuple-element.19.refs_5_.refs_8_.refs_10_), channel_id=1, source_target_pairs={{0,2},{2,0},{4,6},{6,4},{1,3},{3,1},{5,7},{7,5},{8,10},{10,8},{12,... | collective-permute-start | bytes 835592 | tf_op jit(solution)/shard_map/ppermute | solution.py:220
  18.7 11.0 %collective-permute-start.8 = (bf16[4,272,128]{2,1,0:T(8,128)(2,1)S(1)}, bf16[4,272,128]{2,1,0:T(8,128)(2,1)S(1)}, u32[]{:S(2)}, u32[]{:S(2)}) collective-permute-start(bf16[4,272,128]{2,1,0:T(8,128)(2,1)S(1)} %get-tuple-element.19.refs_5_.refs_8_.refs_10_), channel_id=1, source_target_pairs={{2,4},{4,2},{3,5},{5,3},{10,12},{12,10},{11,13},{13,11},{18,20},{2... | collective-permute-start | bytes 835592 | tf_op jit(solution)/shard_map/ppermute | solution.py:219
  20.6 11.3 %collective-permute-start.7 = (bf16[4,192,128]{2,1,0:T(8,128)(2,1)S(1)}, bf16[4,192,128]{2,1,0:T(8,128)(2,1)S(1)}, u32[]{:S(2)}, u32[]{:S(2)}) collective-permute-start(bf16[4,192,128]{2,1,0:T(8,128)(2,1)S(1)} %get-tuple-element.18.refs_5_.refs_8_), channel_id=1, source_target_pairs={{0,2},{2,0},{4,6},{6,4},{1,3},{3,1},{5,7},{7,5},{8,10},{10,8},{12,... | collective-permute-start | bytes 589832 | tf_op jit(solution)/shard_map/ppermute | solution.py:220
  24.4 7.5 %collective-permute-start.6 = (bf16[4,192,128]{2,1,0:T(8,128)(2,1)S(1)}, bf16[4,192,128]{2,1,0:T(8,128)(2,1)S(1)}, u32[]{:S(2)}, u32[]{:S(2)}) collective-permute-start(bf16[4,192,128]{2,1,0:T(8,128)(2,1)S(1)} %get-tuple-element.18.refs_5_.refs_8_), channel_id=1, source_target_pairs={{2,4},{4,2},{3,5},{5,3},{10,12},{12,10},{11,13},{13,11},{18,20},{2... | collective-permute-start | bytes 589832 | tf_op jit(solution)/shard_map/ppermute | solution.py:219
  25.8 8.0 %collective-permute-start.5 = (bf16[4,112,128]{2,1,0:T(8,128)(2,1)S(1)}, bf16[4,112,128]{2,1,0:T(8,128)(2,1)S(1)}, u32[]{:S(2)}, u32[]{:S(2)}) collective-permute-start(bf16[4,112,128]{2,1,0:T(8,128)(2,1)S(1)} %shard_map.67.refs_5_), channel_id=1, source_target_pairs={{0,2},{2,0},{4,6},{6,4},{1,3},{3,1},{5,7},{7,5},{8,10},{10,8},{12,... | collective-permute-start | bytes 344072 | tf_op jit(solution)/shard_map/ppermute | solution.py:220
  29.1 4.8 %collective-permute-start.4 = (bf16[4,112,128]{2,1,0:T(8,128)(2,1)S(1)}, bf16[4,112,128]{2,1,0:T(8,128)(2,1)S(1)}, u32[]{:S(2)}, u32[]{:S(2)}) collective-permute-start(bf16[4,112,128]{2,1,0:T(8,128)(2,1)S(1)} %shard_map.67.refs_5_), channel_id=1, source_target_pairs={{2,4},{4,2},{3,5},{5,3},{10,12},{12,10},{11,13},{13,11},{18,20},{2... | collective-permute-start | bytes 344072 | tf_op jit(solution)/shard_map/ppermute | solution.py:219
where the time goes:
time: 35.7 us; the launch traced here: 35.4 us
  starting transfers between devices  22.4 us (63%)
  Pallas kernels  9.19 us (26%)
  local copies, waits for them, and re-layouts  3.53 us (10%)
    ppermute x5, starting transfers between devices, member_step(): even_swap = lax.ppermute(own, 'band', even_pairs)  19.1 us
    pallas_call x6, Pallas kernels, layer_chunk(): pl.pallas_call(functools.partial(chunk_kernel, layer, first, last, offset...  9.17 us
    ppermute x5, starting transfers between devices, member_step(): odd_swap = lax.ppermute(own, 'band', odd_pairs)  3.32 us
    unnamed x16, local copies, waits for them, and re-layouts  2.47 us
    slice x1, local copies, waits for them, and re-layouts, member_step(): chunks = [state[:, :ranges[0][1]]]  1.06 us
  transfers between devices with their start and end apart: 10, of which 0 were waited for; matrix products, arithmetic and copies ran while one was open for 0% of the time, Pallas kernels for 22%

commit v1 on v0

--- a/solution.py
+++ b/solution.py
@@ -36,7 +36,7 @@
     )(state, *after)
 
 
-def chunk_kernel(layer, first, last, offset, width, prev_end, place, *refs):
+def chunk_kernel(layer, first, last, offset, width, prev_end, place, earlier, *refs):
     refs = list(refs)
     lat_w, lon_w, gain, w_in, w_out, own, odd_swap, even_swap = refs[:8]
     refs = refs[8:]
@@ -46,8 +46,7 @@
     if last and not first:
         first_own, first_mix = refs[:2]
         refs = refs[2:]
-    if place is not None and not first:
-        refs.pop(0)
+    results, refs = refs[: len(earlier)], refs[len(earlier) :]
     out = refs.pop(0)
     if not last:
         tail = refs.pop(0)
@@ -55,8 +54,13 @@
         head = refs.pop(0)
     mix, state = refs[:2]
     whole = out
+    copies = []
     if place is not None:
         out, sems = refs[2:]
+        for to, result in zip(earlier, results):
+            there = whole.at[:, to : to + result.shape[1]]
+            copies.append(pltpu.make_async_copy(result, there, sems.at[len(copies)]))
+            copies[-1].start()
     rows = own.shape[0]
     channels = own.shape[2]
     start = 0 if first else 2 * PAD
@@ -90,7 +94,7 @@
             state[r, pl.ds(to, PAD)] = mine[r]
         return carry
 
-    lax.fori_loop(0, width // PAD, mix_tile, 0, unroll=2)
+    lax.fori_loop(0, width // PAD, mix_tile, 0, unroll=4)
 
     if not last:
         tail[...] = mix[:, start + width - 2 * PAD : start + width].astype(jnp.bfloat16)
@@ -124,7 +128,6 @@
             new = state[r, pl.ds(at + PAD, tile)].astype(jnp.float32) + delta[r * tile : (r + 1) * tile]
             out[r, pl.ds(at, tile)] = new.astype(jnp.bfloat16)
 
-    copies = []
     for at, tile in tiles(made, total, place):
         rest(at, tile)
         if place is not None:
@@ -145,7 +148,7 @@
     return [(lo, hi - lo) for lo, hi in zip(edges[:-1], edges[1:])]
 
 
-def layer_chunk(layer, weights, chunk, offset, width, prev, first_chunk, first, last, place=None, whole=None):
+def layer_chunk(layer, weights, chunk, offset, width, prev, first_chunk, first, last, place=None, lons=None, earlier=()):
     own = chunk[0]
     rows, _, channels = own.shape
     prev_end = None if first else prev[1]
@@ -164,16 +167,13 @@
         pltpu.VMEM((rows, window, channels), jnp.float32),
         pltpu.VMEM((rows, window, channels), jnp.bfloat16),
     ]
-    aliases = {}
     if place is not None:
-        lons = whole if first else whole.shape[1]
-        scratch += [pltpu.VMEM(outs[0].shape, jnp.bfloat16), pltpu.SemaphoreType.DMA((len(tiles(made, lons, place)),))]
+        sems = len(earlier) + len(tiles(made, lons, place))
+        scratch += [pltpu.VMEM(outs[0].shape, jnp.bfloat16), pltpu.SemaphoreType.DMA((sems,))]
         outs = [jax.ShapeDtypeStruct((rows, lons, channels), jnp.bfloat16)]
         out_specs = [pl.BlockSpec(memory_space=pltpu.HBM)]
-        if not first:
-            aliases = {len(args): 0}
-            args.append(whole)
-            specs += out_specs
+        args += [result for _, result in earlier]
+        specs += [pl.BlockSpec(memory_space=pltpu.VMEM)] * len(earlier)
     if not last:
         outs.append(strip)
     if first and not last:
@@ -182,12 +182,11 @@
     cells = rows * made
     hidden = weights[3].shape[2]
     return pl.pallas_call(
-        functools.partial(chunk_kernel, layer, first, last, offset, width, prev_end, place),
+        functools.partial(chunk_kernel, layer, first, last, offset, width, prev_end, place, [at for at, _ in earlier]),
         out_shape=outs,
         in_specs=specs,
         out_specs=out_specs,
         scratch_shapes=scratch,
-        input_output_aliases=aliases,
         compiler_params=pltpu.CompilerParams(vmem_limit_bytes=24 * 2**20),
         cost_estimate=pl.CostEstimate(
             flops=50 * cells * channels * hidden, bytes_accessed=8 * cells * channels, transcendentals=cells * hidden
@@ -212,7 +211,7 @@
     chunks = [state[:, : ranges[0][1]]]
     for lo, hi in ranges[1:]:
         chunks.append(later_columns(state, lo, hi, weights))
-    whole, place = lons, LAYERS * PAD
+    place, earlier = LAYERS * PAD, []
     for layer in range(LAYERS):
         halos = []
         for own in chunks:
@@ -229,20 +228,20 @@
         for p, (c, offset, width) in enumerate(pieces):
             own = chunks[c]
             first, last = p == 0, p == len(pieces) - 1
-            where = (place, whole) if final else ()
+            where = (place, lons, earlier) if final and last else ()
             got = layer_chunk(
                 layer, weights, (own,) + halos[c], offset, width, prev, first_chunk, first, last, *where
             )
             made.append(got[0])
             if final:
-                whole = got[0]
-                place += width - (2 * PAD if first else 0)
+                earlier.append((place, got[0]))
+                place += got[0].shape[1]
             if not last:
                 prev = (own, offset + width, got[1])
             if first and not last:
                 first_chunk = (own, got[2])
         chunks = made
-    return whole
+    return chunks[-1]
 
 
 def solution(mesh):

time: 35.7 us -> 34.6 us (0.969)
  Pallas kernels: 9.19 us -> 7.77 us
    pallas_call x6, Pallas kernels: 9.17 us -> 7.75 us  [layer_chunk(): pl.pallas_call(functools.partial(chunk_kernel, layer, first, last, offset...]
  transfers between devices with their start and end apart: 10 -> 10, of which waited for: 0 -> 0; matrix products, arithmetic and copies ran while one was open for 0% -> 0% of each run, Pallas kernels for 22% -> 18%
where the time goes in v1:
time: 34.6 us; the launch traced here: 34 us
  starting transfers between devices  22.5 us (65%)
  Pallas kernels  7.77 us (22%)
  local copies, waits for them, and re-layouts  3.53 us (10%)
    ppermute x5, starting transfers between devices, member_step(): even_swap = lax.ppermute(own, 'band', even_pairs)  19.2 us
    pallas_call x6, Pallas kernels, layer_chunk(): pl.pallas_call(functools.partial(chunk_kernel, layer, first, last, offset...  7.75 us
    ppermute x5, starting transfers between devices, member_step(): odd_swap = lax.ppermute(own, 'band', odd_pairs)  3.32 us
    unnamed x16, local copies, waits for them, and re-layouts  2.47 us
    slice x1, local copies, waits for them, and re-layouts, member_step(): chunks = [state[:, :ranges[0][1]]]  1.06 us
  transfers between devices with their start and end apart: 10, of which 0 were waited for; matrix products, arithmetic and copies ran while one was open for 0% of the time, Pallas kernels for 18%

profile of v1, /device:TPU:0, one launch (start us, length us, event | category | flops | bytes accessed | tf_op | source)
XLA Modules:
  0.0 34.0 jit_solution(11737738789982541529)
XLA Ops:
  0.0 1.1 %slice.4.refs_5_.refs_8_.refs_10_ = bf16[4,304,128]{2,1,0:T(8,128)(2,1)S(1)} slice(bf16[4,576,128]{2,1,0:T(8,128)(2,1)} %bitcast.4), slice={[0:4], [0:304], [0:128]} | slice | bytes 622592 | tf_op jit(solution)/shard_map/slice | solution.py:211
  1.1 3.1 %collective-permute-start.3 = (bf16[4,304,128]{2,1,0:T(8,128)(2,1)S(1)}, bf16[4,304,128]{2,1,0:T(8,128)(2,1)S(1)}, u32[]{:S(2)}, u32[]{:S(2)}) collective-permute-start(bf16[4,304,128]{2,1,0:T(8,128)(2,1)S(1)} %slice.4.refs_5_.refs_8_.refs_10_), channel_id=1, source_target_pairs={{0,2},{2,0},{4,6},{6,4},{1,3},{3,1},{5,7},{7,5},{8,10},{10,8},{12,... | collective-permute-start | bytes 933896 | tf_op jit(solution)/shard_map/ppermute | solution.py:219
  4.2 0.7 %collective-permute-start.2 = (bf16[4,304,128]{2,1,0:T(8,128)(2,1)S(1)}, bf16[4,304,128]{2,1,0:T(8,128)(2,1)S(1)}, u32[]{:S(2)}, u32[]{:S(2)}) collective-permute-start(bf16[4,304,128]{2,1,0:T(8,128)(2,1)S(1)} %slice.4.refs_5_.refs_8_.refs_10_), channel_id=1, source_target_pairs={{2,4},{4,2},{3,5},{5,3},{10,12},{12,10},{11,13},{13,11},{18,20},{2... | collective-permute-start | bytes 933896 | tf_op jit(solution)/shard_map/ppermute | solution.py:218
  4.8 0.0 copy-start.7
  4.9 0.6 %copy-done.7 = f32[2,128]{1,0:T(2,128)S(1)} copy-done((f32[2,128]{1,0:T(2,128)S(1)}, f32[2,128]{1,0:T(2,128)}, u32[]{:S(2)}) %copy-start.7) | copy-done | bytes 1048
  5.5 0.9 %copy-done.1 = bf16[2,128,256]{2,1,0:T(8,128)(2,1)S(1)} copy-done((bf16[2,128,256]{2,1,0:T(8,128)(2,1)S(1)}, bf16[2,128,256]{2,1,0:T(8,128)(2,1)}, u32[]{:S(2)}) %copy-start.1) | copy-done | bytes 131096
  6.4 0.9 %copy-done.3 = bf16[2,256,128]{2,1,0:T(8,128)(2,1)S(1)} copy-done((bf16[2,256,128]{2,1,0:T(8,128)(2,1)S(1)}, bf16[2,256,128]{2,1,0:T(8,128)(2,1)}, u32[]{:S(2)}) %copy-start.3) | copy-done | bytes 131096
  7.3 4.4 %collective-permute-start.1 = (bf16[4,272,128]{2,1,0:T(8,128)(2,1)S(1)}, bf16[4,272,128]{2,1,0:T(8,128)(2,1)S(1)}, u32[]{:S(2)}, u32[]{:S(2)}) collective-permute-start(bf16[4,272,128]{2,1,0:T(8,128)(2,1)S(1)} %shard_map.64.refs_5_.refs_8_), channel_id=1, source_target_pairs={{0,2},{2,0},{4,6},{6,4},{1,3},{3,1},{5,7},{7,5},{8,10},{10,8},{12,... | collective-permute-start | bytes 835592 | tf_op jit(solution)/shard_map/ppermute | solution.py:219
  11.8 0.7 %collective-permute-start = (bf16[4,272,128]{2,1,0:T(8,128)(2,1)S(1)}, bf16[4,272,128]{2,1,0:T(8,128)(2,1)S(1)}, u32[]{:S(2)}, u32[]{:S(2)}) collective-permute-start(bf16[4,272,128]{2,1,0:T(8,128)(2,1)S(1)} %shard_map.64.refs_5_.refs_8_), channel_id=1, source_target_pairs={{2,4},{4,2},{3,5},{5,3},{10,12},{12,10},{11,13},{13,11},{18,20},{2... | collective-permute-start | bytes 835592 | tf_op jit(solution)/shard_map/ppermute | solution.py:218
  12.5 0.0 collective-permute-done.3.refs_7_
  12.5 1.6 %shard_map.65 = (bf16[4,272,128]{2,1,0:T(8,128)(2,1)S(1)}, bf16[4,32,128]{2,1,0:T(8,128)(2,1)S(1)}, bf16[4,32,128]{2,1,0:T(8,128)(2,1)S(1)}) custom-call(bf16[9,2,128]{2,1,0:T(2,128)(2,1)S(1)} %bitcast.7, bf16[9,2,128]{2,1,0:T(2,128)(2,1)S(1)} %bitcast.14, f32[2,128]{1,0:T(2,128)S(1)} %copy-done.7, bf16[2,128,256]{2,1,0:T(8,128)(2,1)S(1)} %copy-done.2, ...), custom_call_target="tpu_custom_call" | custom-call | flops 1782579200 | bytes 1114112 | tf_op jit(solution)/shard_map/pallas_call | solution.py:184
  14.1 4.5 %collective-permute-start.9 = (bf16[4,272,128]{2,1,0:T(8,128)(2,1)S(1)}, bf16[4,272,128]{2,1,0:T(8,128)(2,1)S(1)}, u32[]{:S(2)}, u32[]{:S(2)}) collective-permute-start(bf16[4,272,128]{2,1,0:T(8,128)(2,1)S(1)} %get-tuple-element.19.refs_5_.refs_8_.refs_10_), channel_id=1, source_target_pairs={{0,2},{2,0},{4,6},{6,4},{1,3},{3,1},{5,7},{7,5},{8,10},{10,8},{12,... | collective-permute-start | bytes 835592 | tf_op jit(solution)/shard_map/ppermute | solution.py:219
  18.7 0.7 %collective-permute-start.8 = (bf16[4,272,128]{2,1,0:T(8,128)(2,1)S(1)}, bf16[4,272,128]{2,1,0:T(8,128)(2,1)S(1)}, u32[]{:S(2)}, u32[]{:S(2)}) collective-permute-start(bf16[4,272,128]{2,1,0:T(8,128)(2,1)S(1)} %get-tuple-element.19.refs_5_.refs_8_.refs_10_), channel_id=1, source_target_pairs={{2,4},{4,2},{3,5},{5,3},{10,12},{12,10},{11,13},{13,11},{18,20},{2... | collective-permute-start | bytes 835592 | tf_op jit(solution)/shard_map/ppermute | solution.py:218
  19.4 1.1 %shard_map.66 = (bf16[4,192,128]{2,1,0:T(8,128)(2,1)S(1)}, bf16[4,32,128]{2,1,0:T(8,128)(2,1)S(1)}) custom-call(bf16[9,2,128]{2,1,0:T(2,128)(2,1)S(1)} %bitcast.8, bf16[9,2,128]{2,1,0:T(2,128)(2,1)S(1)} %bitcast.15, f32[2,128]{1,0:T(2,128)S(1)} %copy-done.7, bf16[2,128,256]{2,1,0:T(8,128)(2,1)S(1)} %copy-done.2, bf16[2,256,128]{2,1,0:T(8,128)(2,1)S(1)} %copy-done.3, ...), custom_call_target="tpu_custom_call" | custom-call | flops 1258291200 | bytes 786432 | tf_op jit(solution)/shard_map/pallas_call | solution.py:184
  20.5 3.8 %collective-permute-start.7 = (bf16[4,192,128]{2,1,0:T(8,128)(2,1)S(1)}, bf16[4,192,128]{2,1,0:T(8,128)(2,1)S(1)}, u32[]{:S(2)}, u32[]{:S(2)}) collective-permute-start(bf16[4,192,128]{2,1,0:T(8,128)(2,1)S(1)} %get-tuple-element.18.refs_5_.refs_8_), channel_id=1, source_target_pairs={{0,2},{2,0},{4,6},{6,4},{1,3},{3,1},{5,7},{7,5},{8,10},{10,8},{12,... | collective-permute-start | bytes 589832 | tf_op jit(solution)/shard_map/ppermute | solution.py:219
  24.3 0.7 %collective-permute-start.6 = (bf16[4,192,128]{2,1,0:T(8,128)(2,1)S(1)}, bf16[4,192,128]{2,1,0:T(8,128)(2,1)S(1)}, u32[]{:S(2)}, u32[]{:S(2)}) collective-permute-start(bf16[4,192,128]{2,1,0:T(8,128)(2,1)S(1)} %get-tuple-element.18.refs_5_.refs_8_), channel_id=1, source_target_pairs={{2,4},{4,2},{3,5},{5,3},{10,12},{12,10},{11,13},{13,11},{18,20},{2... | collective-permute-start | bytes 589832 | tf_op jit(solution)/shard_map/ppermute | solution.py:218
  25.0 0.0 copy-start.4
  25.0 0.8 %shard_map.67.refs_5_ = bf16[4,112,128]{2,1,0:T(8,128)(2,1)S(1)} custom-call(bf16[9,2,128]{2,1,0:T(2,128)(2,1)S(1)} %bitcast.9, bf16[9,2,128]{2,1,0:T(2,128)(2,1)S(1)} %bitcast.16, f32[2,128]{1,0:T(2,128)S(1)} %copy-done.7, bf16[2,128,256]{2,1,0:T(8,128)(2,1)S(1)} %copy-done.2, bf16[2,256,128]{2,1,0:T(8,128)(2,1)S(1)} %copy-done.3, ...), custom_call_target="tpu_custom_call" | custom-call | flops 734003200 | bytes 458752 | tf_op jit(solution)/shard_map/pallas_call | solution.py:184
  25.8 3.3 %collective-permute-start.5 = (bf16[4,112,128]{2,1,0:T(8,128)(2,1)S(1)}, bf16[4,112,128]{2,1,0:T(8,128)(2,1)S(1)}, u32[]{:S(2)}, u32[]{:S(2)}) collective-permute-start(bf16[4,112,128]{2,1,0:T(8,128)(2,1)S(1)} %shard_map.67.refs_5_), channel_id=1, source_target_pairs={{0,2},{2,0},{4,6},{6,4},{1,3},{3,1},{5,7},{7,5},{8,10},{10,8},{12,... | collective-permute-start | bytes 344072 | tf_op jit(solution)/shard_map/ppermute | solution.py:219
  29.1 0.7 %collective-permute-start.4 = (bf16[4,112,128]{2,1,0:T(8,128)(2,1)S(1)}, bf16[4,112,128]{2,1,0:T(8,128)(2,1)S(1)}, u32[]{:S(2)}, u32[]{:S(2)}) collective-permute-start(bf16[4,112,128]{2,1,0:T(8,128)(2,1)S(1)} %shard_map.67.refs_5_), channel_id=1, source_target_pairs={{2,4},{4,2},{3,5},{5,3},{10,12},{12,10},{11,13},{13,11},{18,20},{2... | collective-permute-start | bytes 344072 | tf_op jit(solution)/shard_map/ppermute | solution.py:218
  29.8 1.5 %shard_map.68 = (bf16[4,240,128]{2,1,0:T(8,128)(2,1)S(1)}, bf16[4,32,128]{2,1,0:T(8,128)(2,1)S(1)}, bf16[4,32,128]{2,1,0:T(8,128)(2,1)S(1)}) custom-call(bf16[9,2,128]{2,1,0:T(2,128)(2,1)S(1)} %bitcast.10, bf16[9,2,128]{2,1,0:T(2,128)(2,1)S(1)} %bitcast.17, f32[2,128]{1,0:T(2,128)S(1)} %copy-done.7, bf16[2,128,256]{2,1,0:T(8,128)(2,1)S(1)} %copy-done.2, ...), custom_call_target="tpu_custom_call" | custom-call | flops 1572864000 | bytes 983040 | tf_op jit(solution)/shard_map/pallas_call | solution.py:184
  31.2 0.0 collective-permute-done.6.refs_6_
  31.2 1.1 %shard_map.69 = (bf16[4,192,128]{2,1,0:T(8,128)(2,1)S(1)}, bf16[4,32,128]{2,1,0:T(8,128)(2,1)S(1)}) custom-call(bf16[9,2,128]{2,1,0:T(2,128)(2,1)S(1)} %bitcast.11, bf16[9,2,128]{2,1,0:T(2,128)(2,1)S(1)} %bitcast.18, f32[2,128]{1,0:T(2,128)S(1)} %copy-done.7, bf16[2,128,256]{2,1,0:T(8,128)(2,1)S(1)} %copy-done.2, bf16[2,256,128]{2,1,0:T(8,128)(2,1)S(1)} %copy-done.4, ...), custom_call_target="tpu_custom_call" | custom-call | flops 1258291200 | bytes 786432 | tf_op jit(solution)/shard_map/pallas_call | solution.py:184
  32.4 1.6 %shard_map.70 = bf16[4,576,128]{2,1,0:T(8,128)(2,1)} custom-call(bf16[9,2,128]{2,1,0:T(2,128)(2,1)S(1)} %bitcast.12, bf16[9,2,128]{2,1,0:T(2,128)(2,1)S(1)} %bitcast.19, f32[2,128]{1,0:T(2,128)S(1)} %copy-done.7, bf16[2,128,256]{2,1,0:T(8,128)(2,1)S(1)} %copy-done.2, bf16[2,256,128]{2,1,0:T(8,128)(2,1)S(1)} %copy-done.4, ...), custom_call_target="tpu_custom_call" | custom-call | flops 943718400 | bytes 589824 | tf_op jit(solution)/shard_map/pallas_call | solution.py:184
  (20 shorter events, 0.1 us)
Async XLA Ops:
  0.0 4.8 %copy-start = (bf16[1,4,576,128]{3,2,1,0:T(8,128)(2,1)S(1)}, bf16[1,4,576,128]{3,2,1,0:T(8,128)(2,1)}, u32[]{:S(2)}) copy-start(bf16[1,4,576,128]{3,2,1,0:T(8,128)(2,1)} %param.6) | copy-start | bytes 1769476
  0.0 4.9 %copy-start.5 = (bf16[2,9,128]{2,0,1:T(2,128)(2,1)S(1)}, bf16[2,9,128]{2,0,1:T(2,128)(2,1)}, u32[]{:S(2)}) copy-start(bf16[2,9,128]{2,0,1:T(2,128)(2,1)} %param.7) | copy-start | bytes 13828
  0.0 4.9 %copy-start.6 = (bf16[2,9,128]{2,0,1:T(2,128)(2,1)S(1)}, bf16[2,9,128]{2,0,1:T(2,128)(2,1)}, u32[]{:S(2)}) copy-start(bf16[2,9,128]{2,0,1:T(2,128)(2,1)} %param.8) | copy-start | bytes 13828
  1.1 11.4 %collective-permute-start.3 = (bf16[4,304,128]{2,1,0:T(8,128)(2,1)S(1)}, bf16[4,304,128]{2,1,0:T(8,128)(2,1)S(1)}, u32[]{:S(2)}, u32[]{:S(2)}) collective-permute-start(bf16[4,304,128]{2,1,0:T(8,128)(2,1)S(1)} %slice.4.refs_5_.refs_8_.refs_10_), channel_id=1, source_target_pairs={{0,2},{2,0},{4,6},{6,4},{1,3},{3,1},{5,7},{7,5},{8,10},{10,8},{12,... | collective-permute-start | bytes 933896 | tf_op jit(solution)/shard_map/ppermute | solution.py:219
  4.2 8.3 %collective-permute-start.2 = (bf16[4,304,128]{2,1,0:T(8,128)(2,1)S(1)}, bf16[4,304,128]{2,1,0:T(8,128)(2,1)S(1)}, u32[]{:S(2)}, u32[]{:S(2)}) collective-permute-start(bf16[4,304,128]{2,1,0:T(8,128)(2,1)S(1)} %slice.4.refs_5_.refs_8_.refs_10_), channel_id=1, source_target_pairs={{2,4},{4,2},{3,5},{5,3},{10,12},{12,10},{11,13},{13,11},{18,20},{2... | collective-permute-start | bytes 933896 | tf_op jit(solution)/shard_map/ppermute | solution.py:218
  4.8 0.7 %copy-start.7 = (f32[2,128]{1,0:T(2,128)S(1)}, f32[2,128]{1,0:T(2,128)}, u32[]{:S(2)}) copy-start(f32[2,128]{1,0:T(2,128)} %refs_2_.13) | copy-start | bytes 3076
  5.5 0.9 %copy-start.1 = (bf16[2,128,256]{2,1,0:T(8,128)(2,1)S(1)}, bf16[2,128,256]{2,1,0:T(8,128)(2,1)}, u32[]{:S(2)}) copy-start(bf16[2,128,256]{2,1,0:T(8,128)(2,1)} %refs_3_.13) | copy-start | bytes 393220
  6.4 0.9 %copy-start.3 = (bf16[2,256,128]{2,1,0:T(8,128)(2,1)S(1)}, bf16[2,256,128]{2,1,0:T(8,128)(2,1)}, u32[]{:S(2)}) copy-start(bf16[2,256,128]{2,1,0:T(8,128)(2,1)} %refs_4_.13) | copy-start | bytes 393220
  7.3 5.2 %copy-start.2 = (bf16[2,128,256]{2,1,0:T(8,128)(2,1)S(1)}, bf16[2,128,256]{2,1,0:T(8,128)(2,1)}, u32[]{:S(2)}) copy-start(bf16[2,128,256]{2,1,0:T(8,128)(2,1)} %refs_3_.13) | copy-start | bytes 393220
  7.3 12.0 %collective-permute-start.1 = (bf16[4,272,128]{2,1,0:T(8,128)(2,1)S(1)}, bf16[4,272,128]{2,1,0:T(8,128)(2,1)S(1)}, u32[]{:S(2)}, u32[]{:S(2)}) collective-permute-start(bf16[4,272,128]{2,1,0:T(8,128)(2,1)S(1)} %shard_map.64.refs_5_.refs_8_), channel_id=1, source_target_pairs={{0,2},{2,0},{4,6},{6,4},{1,3},{3,1},{5,7},{7,5},{8,10},{10,8},{12,... | collective-permute-start | bytes 835592 | tf_op jit(solution)/shard_map/ppermute | solution.py:219
  11.8 7.5 %collective-permute-start = (bf16[4,272,128]{2,1,0:T(8,128)(2,1)S(1)}, bf16[4,272,128]{2,1,0:T(8,128)(2,1)S(1)}, u32[]{:S(2)}, u32[]{:S(2)}) collective-permute-start(bf16[4,272,128]{2,1,0:T(8,128)(2,1)S(1)} %shard_map.64.refs_5_.refs_8_), channel_id=1, source_target_pairs={{2,4},{4,2},{3,5},{5,3},{10,12},{12,10},{11,13},{13,11},{18,20},{2... | collective-permute-start | bytes 835592 | tf_op jit(solution)/shard_map/ppermute | solution.py:218
  14.1 15.0 %collective-permute-start.9 = (bf16[4,272,128]{2,1,0:T(8,128)(2,1)S(1)}, bf16[4,272,128]{2,1,0:T(8,128)(2,1)S(1)}, u32[]{:S(2)}, u32[]{:S(2)}) collective-permute-start(bf16[4,272,128]{2,1,0:T(8,128)(2,1)S(1)} %get-tuple-element.19.refs_5_.refs_8_.refs_10_), channel_id=1, source_target_pairs={{0,2},{2,0},{4,6},{6,4},{1,3},{3,1},{5,7},{7,5},{8,10},{10,8},{12,... | collective-permute-start | bytes 835592 | tf_op jit(solution)/shard_map/ppermute | solution.py:219
  18.7 11.1 %collective-permute-start.8 = (bf16[4,272,128]{2,1,0:T(8,128)(2,1)S(1)}, bf16[4,272,128]{2,1,0:T(8,128)(2,1)S(1)}, u32[]{:S(2)}, u32[]{:S(2)}) collective-permute-start(bf16[4,272,128]{2,1,0:T(8,128)(2,1)S(1)} %get-tuple-element.19.refs_5_.refs_8_.refs_10_), channel_id=1, source_target_pairs={{2,4},{4,2},{3,5},{5,3},{10,12},{12,10},{11,13},{13,11},{18,20},{2... | collective-permute-start | bytes 835592 | tf_op jit(solution)/shard_map/ppermute | solution.py:218
  20.5 10.7 %collective-permute-start.7 = (bf16[4,192,128]{2,1,0:T(8,128)(2,1)S(1)}, bf16[4,192,128]{2,1,0:T(8,128)(2,1)S(1)}, u32[]{:S(2)}, u32[]{:S(2)}) collective-permute-start(bf16[4,192,128]{2,1,0:T(8,128)(2,1)S(1)} %get-tuple-element.18.refs_5_.refs_8_), channel_id=1, source_target_pairs={{0,2},{2,0},{4,6},{6,4},{1,3},{3,1},{5,7},{7,5},{8,10},{10,8},{12,... | collective-permute-start | bytes 589832 | tf_op jit(solution)/shard_map/ppermute | solution.py:219
  24.3 6.9 %collective-permute-start.6 = (bf16[4,192,128]{2,1,0:T(8,128)(2,1)S(1)}, bf16[4,192,128]{2,1,0:T(8,128)(2,1)S(1)}, u32[]{:S(2)}, u32[]{:S(2)}) collective-permute-start(bf16[4,192,128]{2,1,0:T(8,128)(2,1)S(1)} %get-tuple-element.18.refs_5_.refs_8_), channel_id=1, source_target_pairs={{2,4},{4,2},{3,5},{5,3},{10,12},{12,10},{11,13},{13,11},{18,20},{2... | collective-permute-start | bytes 589832 | tf_op jit(solution)/shard_map/ppermute | solution.py:218
  25.0 4.8 %copy-start.4 = (bf16[2,256,128]{2,1,0:T(8,128)(2,1)S(1)}, bf16[2,256,128]{2,1,0:T(8,128)(2,1)}, u32[]{:S(2)}) copy-start(bf16[2,256,128]{2,1,0:T(8,128)(2,1)} %refs_4_.13) | copy-start | bytes 393220
  25.8 6.6 %collective-permute-start.5 = (bf16[4,112,128]{2,1,0:T(8,128)(2,1)S(1)}, bf16[4,112,128]{2,1,0:T(8,128)(2,1)S(1)}, u32[]{:S(2)}, u32[]{:S(2)}) collective-permute-start(bf16[4,112,128]{2,1,0:T(8,128)(2,1)S(1)} %shard_map.67.refs_5_), channel_id=1, source_target_pairs={{0,2},{2,0},{4,6},{6,4},{1,3},{3,1},{5,7},{7,5},{8,10},{10,8},{12,... | collective-permute-start | bytes 344072 | tf_op jit(solution)/shard_map/ppermute | solution.py:219
  29.1 3.3 %collective-permute-start.4 = (bf16[4,112,128]{2,1,0:T(8,128)(2,1)S(1)}, bf16[4,112,128]{2,1,0:T(8,128)(2,1)S(1)}, u32[]{:S(2)}, u32[]{:S(2)}) collective-permute-start(bf16[4,112,128]{2,1,0:T(8,128)(2,1)S(1)} %shard_map.67.refs_5_), channel_id=1, source_target_pairs={{2,4},{4,2},{3,5},{5,3},{10,12},{12,10},{11,13},{13,11},{18,20},{2... | collective-permute-start | bytes 344072 | tf_op jit(solution)/shard_map/ppermute | solution.py:218

commit v2 on v1

--- a/solution.py
+++ b/solution.py
@@ -38,7 +38,7 @@
 
 def chunk_kernel(layer, first, last, offset, width, prev_end, place, earlier, *refs):
     refs = list(refs)
-    lat_w, lon_w, gain, w_in, w_out, own, odd_swap, even_swap = refs[:8]
+    lat_w, lon_w, gain, w_in, w_out, own, even_swap, odd_swap = refs[:8]
     refs = refs[8:]
     if not first:
         prev_own, prev_mix = refs[:2]
@@ -217,13 +217,9 @@
         for own in chunks:
             odd_swap = lax.ppermute(own, "band", odd_pairs)
             even_swap = lax.ppermute(own, "band", even_pairs)
-            halos.append((odd_swap, even_swap))
+            halos.append((even_swap, odd_swap))
         final = layer == LAYERS - 1
         pieces = [(c, 0, own.shape[1]) for c, own in enumerate(chunks)]
-        if layer == 0:
-            c, _, width = pieces.pop()
-            cut = 2 * PAD * (width * 3 // (8 * PAD))
-            pieces += [(c, 0, cut), (c, cut, width - cut)]
         made, prev, first_chunk = [], None, None
         for p, (c, offset, width) in enumerate(pieces):
             own = chunks[c]

time: 34.6 us -> 34.8 us (level)
  the two profiles are of different devices: /device:TPU:0 before, /device:TPU:18 now
where the time goes in v2:
time: 34.8 us; the launch traced here: 34.5 us
  waiting for transfers between devices  12.1 us (35%)
  starting transfers between devices  11.6 us (33%)
  Pallas kernels  7.2 us (21%)
  local copies, waits for them, and re-layouts  3.53 us (10%)
    ppermute x4, waiting for transfers between devices, member_step(): odd_swap = lax.ppermute(own, 'band', odd_pairs)  10.2 us
    ppermute x4, starting transfers between devices, member_step(): odd_swap = lax.ppermute(own, 'band', odd_pairs)  9.72 us
    pallas_call x4, Pallas kernels, layer_chunk(): pl.pallas_call(functools.partial(chunk_kernel, layer, first, last, offset...  7.18 us
    unnamed x16, local copies, waits for them, and re-layouts  2.47 us
    ppermute x4, waiting for transfers between devices, member_step(): even_swap = lax.ppermute(own, 'band', even_pairs)  1.94 us
    ppermute x4, starting transfers between devices, member_step(): even_swap = lax.ppermute(own, 'band', even_pairs)  1.85 us
    slice x1, local copies, waits for them, and re-layouts, member_step(): chunks = [state[:, :ranges[0][1]]]  1.05 us
  transfers between devices with their start and end apart: 8, of which 5 were waited for; matrix products, arithmetic and copies ran while one was open for 0% of the time, Pallas kernels for 14%

profile of v2, /device:TPU:18, one launch (start us, length us, event | category | flops | bytes accessed | tf_op | source)
XLA Modules:
  0.0 34.5 jit_solution(5141749137296888213)
XLA Ops:
  0.0 1.1 %slice.4.refs_5_.refs_8_.refs_10_ = bf16[4,304,128]{2,1,0:T(8,128)(2,1)S(1)} slice(bf16[4,576,128]{2,1,0:T(8,128)(2,1)} %bitcast.4), slice={[0:4], [0:304], [0:128]} | slice | bytes 622592 | tf_op jit(solution)/shard_map/slice | solution.py:211
  1.1 1.6 %collective-permute-start.2 = (bf16[4,304,128]{2,1,0:T(8,128)(2,1)S(1)}, bf16[4,304,128]{2,1,0:T(8,128)(2,1)S(1)}, u32[]{:S(2)}, u32[]{:S(2)}) collective-permute-start(bf16[4,304,128]{2,1,0:T(8,128)(2,1)S(1)} %slice.4.refs_5_.refs_8_.refs_10_), channel_id=1, source_target_pairs={{0,2},{2,0},{4,6},{6,4},{1,3},{3,1},{5,7},{7,5},{8,10},{10,8},{12,... | collective-permute-start | bytes 933896 | tf_op jit(solution)/shard_map/ppermute | solution.py:219
  2.7 1.9 %collective-permute-start.3 = (bf16[4,304,128]{2,1,0:T(8,128)(2,1)S(1)}, bf16[4,304,128]{2,1,0:T(8,128)(2,1)S(1)}, u32[]{:S(2)}, u32[]{:S(2)}) collective-permute-start(bf16[4,304,128]{2,1,0:T(8,128)(2,1)S(1)} %slice.4.refs_5_.refs_8_.refs_10_), channel_id=1, source_target_pairs={{2,4},{4,2},{3,5},{5,3},{10,12},{12,10},{11,13},{13,11},{18,20},{2... | collective-permute-start | bytes 933896 | tf_op jit(solution)/shard_map/ppermute | solution.py:218
  4.6 0.0 copy-start.7
  4.7 0.6 %copy-done.7 = f32[2,128]{1,0:T(2,128)S(1)} copy-done((f32[2,128]{1,0:T(2,128)S(1)}, f32[2,128]{1,0:T(2,128)}, u32[]{:S(2)}) %copy-start.7) | copy-done | bytes 1048
  5.3 0.9 %copy-done.1 = bf16[2,128,256]{2,1,0:T(8,128)(2,1)S(1)} copy-done((bf16[2,128,256]{2,1,0:T(8,128)(2,1)S(1)}, bf16[2,128,256]{2,1,0:T(8,128)(2,1)}, u32[]{:S(2)}) %copy-start.1) | copy-done | bytes 131096
  6.2 0.9 %copy-done.3 = bf16[2,256,128]{2,1,0:T(8,128)(2,1)S(1)} copy-done((bf16[2,256,128]{2,1,0:T(8,128)(2,1)S(1)}, bf16[2,256,128]{2,1,0:T(8,128)(2,1)}, u32[]{:S(2)}) %copy-start.3) | copy-done | bytes 131096
  7.1 0.0 copy-start.4
  7.2 0.1 collective-permute-start
  7.2 3.9 %collective-permute-start.1 = (bf16[4,272,128]{2,1,0:T(8,128)(2,1)S(1)}, bf16[4,272,128]{2,1,0:T(8,128)(2,1)S(1)}, u32[]{:S(2)}, u32[]{:S(2)}) collective-permute-start(bf16[4,272,128]{2,1,0:T(8,128)(2,1)S(1)} %shard_map.64.refs_5_), channel_id=1, source_target_pairs={{2,4},{4,2},{3,5},{5,3},{10,12},{12,10},{11,13},{13,11},{18,20},{2... | collective-permute-start | bytes 835592 | tf_op jit(solution)/shard_map/ppermute | solution.py:218
  11.2 0.0 collective-permute-done.2.refs_6_
  11.2 3.7 %collective-permute-done.3.refs_7_ = bf16[4,304,128]{2,1,0:T(8,128)(2,1)S(1)} collective-permute-done((bf16[4,304,128]{2,1,0:T(8,128)(2,1)S(1)}, bf16[4,304,128]{2,1,0:T(8,128)(2,1)S(1)}, u32[]{:S(2)}, u32[]{:S(2)}) %collective-permute-start.3) | collective-permute-done | bytes 311328 | tf_op jit(solution)/shard_map/ppermute | solution.py:218
  14.9 1.6 %shard_map.65 = (bf16[4,272,128]{2,1,0:T(8,128)(2,1)S(1)}, bf16[4,32,128]{2,1,0:T(8,128)(2,1)S(1)}, bf16[4,32,128]{2,1,0:T(8,128)(2,1)S(1)}) custom-call(bf16[9,2,128]{2,1,0:T(2,128)(2,1)S(1)} %bitcast.7, bf16[9,2,128]{2,1,0:T(2,128)(2,1)S(1)} %bitcast.12, f32[2,128]{1,0:T(2,128)S(1)} %copy-done.7, bf16[2,128,256]{2,1,0:T(8,128)(2,1)S(1)} %copy-done.2, ...), custom_call_target="tpu_custom_call" | custom-call | flops 1782579200 | bytes 1114112 | tf_op jit(solution)/shard_map/pallas_call | solution.py:184
  16.5 0.1 collective-permute-start.6
  16.6 1.9 %collective-permute-start.7 = (bf16[4,272,128]{2,1,0:T(8,128)(2,1)S(1)}, bf16[4,272,128]{2,1,0:T(8,128)(2,1)S(1)}, u32[]{:S(2)}, u32[]{:S(2)}) collective-permute-start(bf16[4,272,128]{2,1,0:T(8,128)(2,1)S(1)} %get-tuple-element.13.refs_5_.refs_8_.refs_10_), channel_id=1, source_target_pairs={{2,4},{4,2},{3,5},{5,3},{10,12},{12,10},{11,13},{13,11},{18,20},{2... | collective-permute-start | bytes 835592 | tf_op jit(solution)/shard_map/ppermute | solution.py:218
  18.5 2.0 %collective-permute-done.1.refs_7_ = bf16[4,272,128]{2,1,0:T(8,128)(2,1)S(1)} collective-permute-done((bf16[4,272,128]{2,1,0:T(8,128)(2,1)S(1)}, bf16[4,272,128]{2,1,0:T(8,128)(2,1)S(1)}, u32[]{:S(2)}, u32[]{:S(2)}) %collective-permute-start.1) | collective-permute-done | bytes 278560 | tf_op jit(solution)/shard_map/ppermute | solution.py:218
  20.5 1.6 %shard_map.66.refs_5_ = bf16[4,304,128]{2,1,0:T(8,128)(2,1)S(1)} custom-call(bf16[9,2,128]{2,1,0:T(2,128)(2,1)S(1)} %bitcast.8, bf16[9,2,128]{2,1,0:T(2,128)(2,1)S(1)} %bitcast.13, f32[2,128]{1,0:T(2,128)S(1)} %copy-done.7, bf16[2,128,256]{2,1,0:T(8,128)(2,1)S(1)} %copy-done.2, bf16[2,256,128]{2,1,0:T(8,128)(2,1)S(1)} %copy-done.4, ...), custom_call_target="tpu_custom_call" | custom-call | flops 1992294400 | bytes 1245184 | tf_op jit(solution)/shard_map/pallas_call | solution.py:184
  22.1 0.1 collective-permute-start.4
  22.2 2.0 %collective-permute-start.5 = (bf16[4,304,128]{2,1,0:T(8,128)(2,1)S(1)}, bf16[4,304,128]{2,1,0:T(8,128)(2,1)S(1)}, u32[]{:S(2)}, u32[]{:S(2)}) collective-permute-start(bf16[4,304,128]{2,1,0:T(8,128)(2,1)S(1)} %shard_map.66.refs_5_), channel_id=1, source_target_pairs={{2,4},{4,2},{3,5},{5,3},{10,12},{12,10},{11,13},{13,11},{18,20},{2... | collective-permute-start | bytes 933896 | tf_op jit(solution)/shard_map/ppermute | solution.py:218
  24.2 2.2 %collective-permute-done.7.refs_7_ = bf16[4,272,128]{2,1,0:T(8,128)(2,1)S(1)} collective-permute-done((bf16[4,272,128]{2,1,0:T(8,128)(2,1)S(1)}, bf16[4,272,128]{2,1,0:T(8,128)(2,1)S(1)}, u32[]{:S(2)}, u32[]{:S(2)}) %collective-permute-start.7) | collective-permute-done | bytes 278560 | tf_op jit(solution)/shard_map/ppermute | solution.py:218
  26.4 1.4 %shard_map.67 = (bf16[4,240,128]{2,1,0:T(8,128)(2,1)S(1)}, bf16[4,32,128]{2,1,0:T(8,128)(2,1)S(1)}, bf16[4,32,128]{2,1,0:T(8,128)(2,1)S(1)}) custom-call(bf16[9,2,128]{2,1,0:T(2,128)(2,1)S(1)} %bitcast.9, bf16[9,2,128]{2,1,0:T(2,128)(2,1)S(1)} %bitcast.14, f32[2,128]{1,0:T(2,128)S(1)} %copy-done.7, bf16[2,128,256]{2,1,0:T(8,128)(2,1)S(1)} %copy-done.2, ...), custom_call_target="tpu_custom_call" | custom-call | flops 1572864000 | bytes 983040 | tf_op jit(solution)/shard_map/pallas_call | solution.py:184
  27.8 1.9 %collective-permute-done.4.refs_6_ = bf16[4,304,128]{2,1,0:T(8,128)(2,1)S(1)} collective-permute-done((bf16[4,304,128]{2,1,0:T(8,128)(2,1)S(1)}, bf16[4,304,128]{2,1,0:T(8,128)(2,1)S(1)}, u32[]{:S(2)}, u32[]{:S(2)}) %collective-permute-start.4) | collective-permute-done | bytes 311328 | tf_op jit(solution)/shard_map/ppermute | solution.py:219
  29.8 2.3 %collective-permute-done.5.refs_7_ = bf16[4,304,128]{2,1,0:T(8,128)(2,1)S(1)} collective-permute-done((bf16[4,304,128]{2,1,0:T(8,128)(2,1)S(1)}, bf16[4,304,128]{2,1,0:T(8,128)(2,1)S(1)}, u32[]{:S(2)}, u32[]{:S(2)}) %collective-permute-start.5) | collective-permute-done | bytes 311328 | tf_op jit(solution)/shard_map/ppermute | solution.py:218
  32.0 2.5 %shard_map.68 = bf16[4,576,128]{2,1,0:T(8,128)(2,1)} custom-call(bf16[9,2,128]{2,1,0:T(2,128)(2,1)S(1)} %bitcast.10, bf16[9,2,128]{2,1,0:T(2,128)(2,1)S(1)} %bitcast.15, f32[2,128]{1,0:T(2,128)S(1)} %copy-done.7, bf16[2,128,256]{2,1,0:T(8,128)(2,1)S(1)} %copy-done.2, bf16[2,256,128]{2,1,0:T(8,128)(2,1)S(1)} %copy-done.4, ...), custom_call_target="tpu_custom_call" | custom-call | flops 2202009600 | bytes 1376256 | tf_op jit(solution)/shard_map/pallas_call | solution.py:184
  (14 shorter events, 0.0 us)
Async XLA Ops:
  0.0 4.6 %copy-start = (bf16[1,4,576,128]{3,2,1,0:T(8,128)(2,1)S(1)}, bf16[1,4,576,128]{3,2,1,0:T(8,128)(2,1)}, u32[]{:S(2)}) copy-start(bf16[1,4,576,128]{3,2,1,0:T(8,128)(2,1)} %param.6) | copy-start | bytes 1769476
  0.0 4.6 %copy-start.5 = (bf16[2,9,128]{2,0,1:T(2,128)(2,1)S(1)}, bf16[2,9,128]{2,0,1:T(2,128)(2,1)}, u32[]{:S(2)}) copy-start(bf16[2,9,128]{2,0,1:T(2,128)(2,1)} %param.7) | copy-start | bytes 13828
  0.0 4.7 %copy-start.6 = (bf16[2,9,128]{2,0,1:T(2,128)(2,1)S(1)}, bf16[2,9,128]{2,0,1:T(2,128)(2,1)}, u32[]{:S(2)}) copy-start(bf16[2,9,128]{2,0,1:T(2,128)(2,1)} %param.8) | copy-start | bytes 13828
  1.1 10.1 %collective-permute-start.2 = (bf16[4,304,128]{2,1,0:T(8,128)(2,1)S(1)}, bf16[4,304,128]{2,1,0:T(8,128)(2,1)S(1)}, u32[]{:S(2)}, u32[]{:S(2)}) collective-permute-start(bf16[4,304,128]{2,1,0:T(8,128)(2,1)S(1)} %slice.4.refs_5_.refs_8_.refs_10_), channel_id=1, source_target_pairs={{0,2},{2,0},{4,6},{6,4},{1,3},{3,1},{5,7},{7,5},{8,10},{10,8},{12,... | collective-permute-start | bytes 933896 | tf_op jit(solution)/shard_map/ppermute | solution.py:219
  2.7 12.2 %collective-permute-start.3 = (bf16[4,304,128]{2,1,0:T(8,128)(2,1)S(1)}, bf16[4,304,128]{2,1,0:T(8,128)(2,1)S(1)}, u32[]{:S(2)}, u32[]{:S(2)}) collective-permute-start(bf16[4,304,128]{2,1,0:T(8,128)(2,1)S(1)} %slice.4.refs_5_.refs_8_.refs_10_), channel_id=1, source_target_pairs={{2,4},{4,2},{3,5},{5,3},{10,12},{12,10},{11,13},{13,11},{18,20},{2... | collective-permute-start | bytes 933896 | tf_op jit(solution)/shard_map/ppermute | solution.py:218
  4.6 0.7 %copy-start.7 = (f32[2,128]{1,0:T(2,128)S(1)}, f32[2,128]{1,0:T(2,128)}, u32[]{:S(2)}) copy-start(f32[2,128]{1,0:T(2,128)} %refs_2_.9) | copy-start | bytes 3076
  5.3 0.9 %copy-start.1 = (bf16[2,128,256]{2,1,0:T(8,128)(2,1)S(1)}, bf16[2,128,256]{2,1,0:T(8,128)(2,1)}, u32[]{:S(2)}) copy-start(bf16[2,128,256]{2,1,0:T(8,128)(2,1)} %refs_3_.9) | copy-start | bytes 393220
  6.2 0.9 %copy-start.3 = (bf16[2,256,128]{2,1,0:T(8,128)(2,1)S(1)}, bf16[2,256,128]{2,1,0:T(8,128)(2,1)}, u32[]{:S(2)}) copy-start(bf16[2,256,128]{2,1,0:T(8,128)(2,1)} %refs_4_.9) | copy-start | bytes 393220
  7.1 7.8 %copy-start.2 = (bf16[2,128,256]{2,1,0:T(8,128)(2,1)S(1)}, bf16[2,128,256]{2,1,0:T(8,128)(2,1)}, u32[]{:S(2)}) copy-start(bf16[2,128,256]{2,1,0:T(8,128)(2,1)} %refs_3_.9) | copy-start | bytes 393220
  7.1 13.3 %copy-start.4 = (bf16[2,256,128]{2,1,0:T(8,128)(2,1)S(1)}, bf16[2,256,128]{2,1,0:T(8,128)(2,1)}, u32[]{:S(2)}) copy-start(bf16[2,256,128]{2,1,0:T(8,128)(2,1)} %refs_4_.9) | copy-start | bytes 393220
  7.2 11.3 %collective-permute-start = (bf16[4,272,128]{2,1,0:T(8,128)(2,1)S(1)}, bf16[4,272,128]{2,1,0:T(8,128)(2,1)S(1)}, u32[]{:S(2)}, u32[]{:S(2)}) collective-permute-start(bf16[4,272,128]{2,1,0:T(8,128)(2,1)S(1)} %shard_map.64.refs_5_), channel_id=1, source_target_pairs={{0,2},{2,0},{4,6},{6,4},{1,3},{3,1},{5,7},{7,5},{8,10},{10,8},{12,... | collective-permute-start | bytes 835592 | tf_op jit(solution)/shard_map/ppermute | solution.py:219
  7.2 13.2 %collective-permute-start.1 = (bf16[4,272,128]{2,1,0:T(8,128)(2,1)S(1)}, bf16[4,272,128]{2,1,0:T(8,128)(2,1)S(1)}, u32[]{:S(2)}, u32[]{:S(2)}) collective-permute-start(bf16[4,272,128]{2,1,0:T(8,128)(2,1)S(1)} %shard_map.64.refs_5_), channel_id=1, source_target_pairs={{2,4},{4,2},{3,5},{5,3},{10,12},{12,10},{11,13},{13,11},{18,20},{2... | collective-permute-start | bytes 835592 | tf_op jit(solution)/shard_map/ppermute | solution.py:218
  16.5 7.7 %collective-permute-start.6 = (bf16[4,272,128]{2,1,0:T(8,128)(2,1)S(1)}, bf16[4,272,128]{2,1,0:T(8,128)(2,1)S(1)}, u32[]{:S(2)}, u32[]{:S(2)}) collective-permute-start(bf16[4,272,128]{2,1,0:T(8,128)(2,1)S(1)} %get-tuple-element.13.refs_5_.refs_8_.refs_10_), channel_id=1, source_target_pairs={{0,2},{2,0},{4,6},{6,4},{1,3},{3,1},{5,7},{7,5},{8,10},{10,8},{12,... | collective-permute-start | bytes 835592 | tf_op jit(solution)/shard_map/ppermute | solution.py:219
  16.6 9.8 %collective-permute-start.7 = (bf16[4,272,128]{2,1,0:T(8,128)(2,1)S(1)}, bf16[4,272,128]{2,1,0:T(8,128)(2,1)S(1)}, u32[]{:S(2)}, u32[]{:S(2)}) collective-permute-start(bf16[4,272,128]{2,1,0:T(8,128)(2,1)S(1)} %get-tuple-element.13.refs_5_.refs_8_.refs_10_), channel_id=1, source_target_pairs={{2,4},{4,2},{3,5},{5,3},{10,12},{12,10},{11,13},{13,11},{18,20},{2... | collective-permute-start | bytes 835592 | tf_op jit(solution)/shard_map/ppermute | solution.py:218
  22.1 7.6 %collective-permute-start.4 = (bf16[4,304,128]{2,1,0:T(8,128)(2,1)S(1)}, bf16[4,304,128]{2,1,0:T(8,128)(2,1)S(1)}, u32[]{:S(2)}, u32[]{:S(2)}) collective-permute-start(bf16[4,304,128]{2,1,0:T(8,128)(2,1)S(1)} %shard_map.66.refs_5_), channel_id=1, source_target_pairs={{0,2},{2,0},{4,6},{6,4},{1,3},{3,1},{5,7},{7,5},{8,10},{10,8},{12,... | collective-permute-start | bytes 933896 | tf_op jit(solution)/shard_map/ppermute | solution.py:219
  22.2 9.8 %collective-permute-start.5 = (bf16[4,304,128]{2,1,0:T(8,128)(2,1)S(1)}, bf16[4,304,128]{2,1,0:T(8,128)(2,1)S(1)}, u32[]{:S(2)}, u32[]{:S(2)}) collective-permute-start(bf16[4,304,128]{2,1,0:T(8,128)(2,1)S(1)} %shard_map.66.refs_5_), channel_id=1, source_target_pairs={{2,4},{4,2},{3,5},{5,3},{10,12},{12,10},{11,13},{13,11},{18,20},{2... | collective-permute-start | bytes 933896 | tf_op jit(solution)/shard_map/ppermute | solution.py:218

commit v3 on v1

--- a/solution.py
+++ b/solution.py
@@ -222,7 +222,7 @@
         pieces = [(c, 0, own.shape[1]) for c, own in enumerate(chunks)]
         if layer == 0:
             c, _, width = pieces.pop()
-            cut = 2 * PAD * (width * 3 // (8 * PAD))
+            cut = 2 * PAD * (5 * width // (12 * PAD))
             pieces += [(c, 0, cut), (c, cut, width - cut)]
         made, prev, first_chunk = [], None, None
         for p, (c, offset, width) in enumerate(pieces):

time: 34.6 us -> 34.4 us (level)
  transfers between devices with their start and end apart: 10 -> 10, of which waited for: 0 -> 0; matrix products, arithmetic and copies ran while one was open for 0% -> 0% of each run, Pallas kernels for 18% -> 19%
where the time goes in v3:
time: 34.4 us; the launch traced here: 34.1 us
  starting transfers between devices  22.5 us (65%)
  Pallas kernels  7.87 us (23%)
  local copies, waits for them, and re-layouts  3.53 us (10%)
    ppermute x5, starting transfers between devices, member_step(): even_swap = lax.ppermute(own, 'band', even_pairs)  19.2 us
    pallas_call x6, Pallas kernels, layer_chunk(): pl.pallas_call(functools.partial(chunk_kernel, layer, first, last, offset...  7.85 us
    ppermute x5, starting transfers between devices, member_step(): odd_swap = lax.ppermute(own, 'band', odd_pairs)  3.32 us
    unnamed x16, local copies, waits for them, and re-layouts  2.47 us
    slice x1, local copies, waits for them, and re-layouts, member_step(): chunks = [state[:, :ranges[0][1]]]  1.06 us
  transfers between devices with their start and end apart: 10, of which 0 were waited for; matrix products, arithmetic and copies ran while one was open for 0% of the time, Pallas kernels for 19%

profile of v3, /device:TPU:0, one launch (start us, length us, event | category | flops | bytes accessed | tf_op | source)
XLA Modules:
  0.0 34.1 jit_solution(12166002169393749530)
XLA Ops:
  0.0 1.1 %slice.4.refs_5_.refs_8_.refs_10_ = bf16[4,304,128]{2,1,0:T(8,128)(2,1)S(1)} slice(bf16[4,576,128]{2,1,0:T(8,128)(2,1)} %bitcast.4), slice={[0:4], [0:304], [0:128]} | slice | bytes 622592 | tf_op jit(solution)/shard_map/slice | solution.py:211
  1.1 3.1 %collective-permute-start.3 = (bf16[4,304,128]{2,1,0:T(8,128)(2,1)S(1)}, bf16[4,304,128]{2,1,0:T(8,128)(2,1)S(1)}, u32[]{:S(2)}, u32[]{:S(2)}) collective-permute-start(bf16[4,304,128]{2,1,0:T(8,128)(2,1)S(1)} %slice.4.refs_5_.refs_8_.refs_10_), channel_id=1, source_target_pairs={{0,2},{2,0},{4,6},{6,4},{1,3},{3,1},{5,7},{7,5},{8,10},{10,8},{12,... | collective-permute-start | bytes 933896 | tf_op jit(solution)/shard_map/ppermute | solution.py:219
  4.2 0.7 %collective-permute-start.2 = (bf16[4,304,128]{2,1,0:T(8,128)(2,1)S(1)}, bf16[4,304,128]{2,1,0:T(8,128)(2,1)S(1)}, u32[]{:S(2)}, u32[]{:S(2)}) collective-permute-start(bf16[4,304,128]{2,1,0:T(8,128)(2,1)S(1)} %slice.4.refs_5_.refs_8_.refs_10_), channel_id=1, source_target_pairs={{2,4},{4,2},{3,5},{5,3},{10,12},{12,10},{11,13},{13,11},{18,20},{2... | collective-permute-start | bytes 933896 | tf_op jit(solution)/shard_map/ppermute | solution.py:218
  4.8 0.0 copy-start.7
  4.9 0.6 %copy-done.7 = f32[2,128]{1,0:T(2,128)S(1)} copy-done((f32[2,128]{1,0:T(2,128)S(1)}, f32[2,128]{1,0:T(2,128)}, u32[]{:S(2)}) %copy-start.7) | copy-done | bytes 1048
  5.5 0.9 %copy-done.1 = bf16[2,128,256]{2,1,0:T(8,128)(2,1)S(1)} copy-done((bf16[2,128,256]{2,1,0:T(8,128)(2,1)S(1)}, bf16[2,128,256]{2,1,0:T(8,128)(2,1)}, u32[]{:S(2)}) %copy-start.1) | copy-done | bytes 131096
  6.4 0.9 %copy-done.3 = bf16[2,256,128]{2,1,0:T(8,128)(2,1)S(1)} copy-done((bf16[2,256,128]{2,1,0:T(8,128)(2,1)S(1)}, bf16[2,256,128]{2,1,0:T(8,128)(2,1)}, u32[]{:S(2)}) %copy-start.3) | copy-done | bytes 131096
  7.3 4.4 %collective-permute-start.1 = (bf16[4,272,128]{2,1,0:T(8,128)(2,1)S(1)}, bf16[4,272,128]{2,1,0:T(8,128)(2,1)S(1)}, u32[]{:S(2)}, u32[]{:S(2)}) collective-permute-start(bf16[4,272,128]{2,1,0:T(8,128)(2,1)S(1)} %shard_map.64.refs_5_.refs_8_), channel_id=1, source_target_pairs={{0,2},{2,0},{4,6},{6,4},{1,3},{3,1},{5,7},{7,5},{8,10},{10,8},{12,... | collective-permute-start | bytes 835592 | tf_op jit(solution)/shard_map/ppermute | solution.py:219
  11.8 0.7 %collective-permute-start = (bf16[4,272,128]{2,1,0:T(8,128)(2,1)S(1)}, bf16[4,272,128]{2,1,0:T(8,128)(2,1)S(1)}, u32[]{:S(2)}, u32[]{:S(2)}) collective-permute-start(bf16[4,272,128]{2,1,0:T(8,128)(2,1)S(1)} %shard_map.64.refs_5_.refs_8_), channel_id=1, source_target_pairs={{2,4},{4,2},{3,5},{5,3},{10,12},{12,10},{11,13},{13,11},{18,20},{2... | collective-permute-start | bytes 835592 | tf_op jit(solution)/shard_map/ppermute | solution.py:218
  12.5 0.0 collective-permute-done.3.refs_7_
  12.5 1.6 %shard_map.65 = (bf16[4,272,128]{2,1,0:T(8,128)(2,1)S(1)}, bf16[4,32,128]{2,1,0:T(8,128)(2,1)S(1)}, bf16[4,32,128]{2,1,0:T(8,128)(2,1)S(1)}) custom-call(bf16[9,2,128]{2,1,0:T(2,128)(2,1)S(1)} %bitcast.7, bf16[9,2,128]{2,1,0:T(2,128)(2,1)S(1)} %bitcast.14, f32[2,128]{1,0:T(2,128)S(1)} %copy-done.7, bf16[2,128,256]{2,1,0:T(8,128)(2,1)S(1)} %copy-done.2, ...), custom_call_target="tpu_custom_call" | custom-call | flops 1782579200 | bytes 1114112 | tf_op jit(solution)/shard_map/pallas_call | solution.py:184
  14.1 4.5 %collective-permute-start.9 = (bf16[4,272,128]{2,1,0:T(8,128)(2,1)S(1)}, bf16[4,272,128]{2,1,0:T(8,128)(2,1)S(1)}, u32[]{:S(2)}, u32[]{:S(2)}) collective-permute-start(bf16[4,272,128]{2,1,0:T(8,128)(2,1)S(1)} %get-tuple-element.19.refs_5_.refs_8_.refs_10_), channel_id=1, source_target_pairs={{0,2},{2,0},{4,6},{6,4},{1,3},{3,1},{5,7},{7,5},{8,10},{10,8},{12,... | collective-permute-start | bytes 835592 | tf_op jit(solution)/shard_map/ppermute | solution.py:219
  18.7 0.7 %collective-permute-start.8 = (bf16[4,272,128]{2,1,0:T(8,128)(2,1)S(1)}, bf16[4,272,128]{2,1,0:T(8,128)(2,1)S(1)}, u32[]{:S(2)}, u32[]{:S(2)}) collective-permute-start(bf16[4,272,128]{2,1,0:T(8,128)(2,1)S(1)} %get-tuple-element.19.refs_5_.refs_8_.refs_10_), channel_id=1, source_target_pairs={{2,4},{4,2},{3,5},{5,3},{10,12},{12,10},{11,13},{13,11},{18,20},{2... | collective-permute-start | bytes 835592 | tf_op jit(solution)/shard_map/ppermute | solution.py:218
  19.4 1.3 %shard_map.66 = (bf16[4,224,128]{2,1,0:T(8,128)(2,1)S(1)}, bf16[4,32,128]{2,1,0:T(8,128)(2,1)S(1)}) custom-call(bf16[9,2,128]{2,1,0:T(2,128)(2,1)S(1)} %bitcast.8, bf16[9,2,128]{2,1,0:T(2,128)(2,1)S(1)} %bitcast.15, f32[2,128]{1,0:T(2,128)S(1)} %copy-done.7, bf16[2,128,256]{2,1,0:T(8,128)(2,1)S(1)} %copy-done.2, bf16[2,256,128]{2,1,0:T(8,128)(2,1)S(1)} %copy-done.3, ...), custom_call_target="tpu_custom_call" | custom-call | flops 1468006400 | bytes 917504 | tf_op jit(solution)/shard_map/pallas_call | solution.py:184
  20.7 3.8 %collective-permute-start.7 = (bf16[4,224,128]{2,1,0:T(8,128)(2,1)S(1)}, bf16[4,224,128]{2,1,0:T(8,128)(2,1)S(1)}, u32[]{:S(2)}, u32[]{:S(2)}) collective-permute-start(bf16[4,224,128]{2,1,0:T(8,128)(2,1)S(1)} %get-tuple-element.18.refs_5_.refs_8_), channel_id=1, source_target_pairs={{0,2},{2,0},{4,6},{6,4},{1,3},{3,1},{5,7},{7,5},{8,10},{10,8},{12,... | collective-permute-start | bytes 688136 | tf_op jit(solution)/shard_map/ppermute | solution.py:219
  24.5 0.7 %collective-permute-start.6 = (bf16[4,224,128]{2,1,0:T(8,128)(2,1)S(1)}, bf16[4,224,128]{2,1,0:T(8,128)(2,1)S(1)}, u32[]{:S(2)}, u32[]{:S(2)}) collective-permute-start(bf16[4,224,128]{2,1,0:T(8,128)(2,1)S(1)} %get-tuple-element.18.refs_5_.refs_8_), channel_id=1, source_target_pairs={{2,4},{4,2},{3,5},{5,3},{10,12},{12,10},{11,13},{13,11},{18,20},{2... | collective-permute-start | bytes 688136 | tf_op jit(solution)/shard_map/ppermute | solution.py:218
  25.2 0.0 copy-start.4
  25.2 0.7 %shard_map.67.refs_5_ = bf16[4,80,128]{2,1,0:T(8,128)(2,1)S(1)} custom-call(bf16[9,2,128]{2,1,0:T(2,128)(2,1)S(1)} %bitcast.9, bf16[9,2,128]{2,1,0:T(2,128)(2,1)S(1)} %bitcast.16, f32[2,128]{1,0:T(2,128)S(1)} %copy-done.7, bf16[2,128,256]{2,1,0:T(8,128)(2,1)S(1)} %copy-done.2, bf16[2,256,128]{2,1,0:T(8,128)(2,1)S(1)} %copy-done.3, ...), custom_call_target="tpu_custom_call" | custom-call | flops 524288000 | bytes 327680 | tf_op jit(solution)/shard_map/pallas_call | solution.py:184
  25.8 3.3 %collective-permute-start.5 = (bf16[4,80,128]{2,1,0:T(8,128)(2,1)S(1)}, bf16[4,80,128]{2,1,0:T(8,128)(2,1)S(1)}, u32[]{:S(2)}, u32[]{:S(2)}) collective-permute-start(bf16[4,80,128]{2,1,0:T(8,128)(2,1)S(1)} %shard_map.67.refs_5_), channel_id=1, source_target_pairs={{0,2},{2,0},{4,6},{6,4},{1,3},{3,1},{5,7},{7,5},{8,10},{10,8},{12,... | collective-permute-start | bytes 245768 | tf_op jit(solution)/shard_map/ppermute | solution.py:219
  29.1 0.7 %collective-permute-start.4 = (bf16[4,80,128]{2,1,0:T(8,128)(2,1)S(1)}, bf16[4,80,128]{2,1,0:T(8,128)(2,1)S(1)}, u32[]{:S(2)}, u32[]{:S(2)}) collective-permute-start(bf16[4,80,128]{2,1,0:T(8,128)(2,1)S(1)} %shard_map.67.refs_5_), channel_id=1, source_target_pairs={{2,4},{4,2},{3,5},{5,3},{10,12},{12,10},{11,13},{13,11},{18,20},{2... | collective-permute-start | bytes 245768 | tf_op jit(solution)/shard_map/ppermute | solution.py:218
  29.8 1.4 %shard_map.68 = (bf16[4,240,128]{2,1,0:T(8,128)(2,1)S(1)}, bf16[4,32,128]{2,1,0:T(8,128)(2,1)S(1)}, bf16[4,32,128]{2,1,0:T(8,128)(2,1)S(1)}) custom-call(bf16[9,2,128]{2,1,0:T(2,128)(2,1)S(1)} %bitcast.10, bf16[9,2,128]{2,1,0:T(2,128)(2,1)S(1)} %bitcast.17, f32[2,128]{1,0:T(2,128)S(1)} %copy-done.7, bf16[2,128,256]{2,1,0:T(8,128)(2,1)S(1)} %copy-done.2, ...), custom_call_target="tpu_custom_call" | custom-call | flops 1572864000 | bytes 983040 | tf_op jit(solution)/shard_map/pallas_call | solution.py:184
  31.3 0.0 collective-permute-done.6.refs_6_
  31.3 1.3 %shard_map.69 = (bf16[4,224,128]{2,1,0:T(8,128)(2,1)S(1)}, bf16[4,32,128]{2,1,0:T(8,128)(2,1)S(1)}) custom-call(bf16[9,2,128]{2,1,0:T(2,128)(2,1)S(1)} %bitcast.11, bf16[9,2,128]{2,1,0:T(2,128)(2,1)S(1)} %bitcast.18, f32[2,128]{1,0:T(2,128)S(1)} %copy-done.7, bf16[2,128,256]{2,1,0:T(8,128)(2,1)S(1)} %copy-done.2, bf16[2,256,128]{2,1,0:T(8,128)(2,1)S(1)} %copy-done.4, ...), custom_call_target="tpu_custom_call" | custom-call | flops 1468006400 | bytes 917504 | tf_op jit(solution)/shard_map/pallas_call | solution.py:184
  32.6 1.5 %shard_map.70 = bf16[4,576,128]{2,1,0:T(8,128)(2,1)} custom-call(bf16[9,2,128]{2,1,0:T(2,128)(2,1)S(1)} %bitcast.12, bf16[9,2,128]{2,1,0:T(2,128)(2,1)S(1)} %bitcast.19, f32[2,128]{1,0:T(2,128)S(1)} %copy-done.7, bf16[2,128,256]{2,1,0:T(8,128)(2,1)S(1)} %copy-done.2, bf16[2,256,128]{2,1,0:T(8,128)(2,1)S(1)} %copy-done.4, ...), custom_call_target="tpu_custom_call" | custom-call | flops 734003200 | bytes 458752 | tf_op jit(solution)/shard_map/pallas_call | solution.py:184
  (20 shorter events, 0.1 us)
Async XLA Ops:
  0.0 4.8 %copy-start = (bf16[1,4,576,128]{3,2,1,0:T(8,128)(2,1)S(1)}, bf16[1,4,576,128]{3,2,1,0:T(8,128)(2,1)}, u32[]{:S(2)}) copy-start(bf16[1,4,576,128]{3,2,1,0:T(8,128)(2,1)} %param.6) | copy-start | bytes 1769476
  0.0 4.9 %copy-start.5 = (bf16[2,9,128]{2,0,1:T(2,128)(2,1)S(1)}, bf16[2,9,128]{2,0,1:T(2,128)(2,1)}, u32[]{:S(2)}) copy-start(bf16[2,9,128]{2,0,1:T(2,128)(2,1)} %param.7) | copy-start | bytes 13828
  0.0 4.9 %copy-start.6 = (bf16[2,9,128]{2,0,1:T(2,128)(2,1)S(1)}, bf16[2,9,128]{2,0,1:T(2,128)(2,1)}, u32[]{:S(2)}) copy-start(bf16[2,9,128]{2,0,1:T(2,128)(2,1)} %param.8) | copy-start | bytes 13828
  1.1 11.4 %collective-permute-start.3 = (bf16[4,304,128]{2,1,0:T(8,128)(2,1)S(1)}, bf16[4,304,128]{2,1,0:T(8,128)(2,1)S(1)}, u32[]{:S(2)}, u32[]{:S(2)}) collective-permute-start(bf16[4,304,128]{2,1,0:T(8,128)(2,1)S(1)} %slice.4.refs_5_.refs_8_.refs_10_), channel_id=1, source_target_pairs={{0,2},{2,0},{4,6},{6,4},{1,3},{3,1},{5,7},{7,5},{8,10},{10,8},{12,... | collective-permute-start | bytes 933896 | tf_op jit(solution)/shard_map/ppermute | solution.py:219
  4.2 8.3 %collective-permute-start.2 = (bf16[4,304,128]{2,1,0:T(8,128)(2,1)S(1)}, bf16[4,304,128]{2,1,0:T(8,128)(2,1)S(1)}, u32[]{:S(2)}, u32[]{:S(2)}) collective-permute-start(bf16[4,304,128]{2,1,0:T(8,128)(2,1)S(1)} %slice.4.refs_5_.refs_8_.refs_10_), channel_id=1, source_target_pairs={{2,4},{4,2},{3,5},{5,3},{10,12},{12,10},{11,13},{13,11},{18,20},{2... | collective-permute-start | bytes 933896 | tf_op jit(solution)/shard_map/ppermute | solution.py:218
  4.8 0.7 %copy-start.7 = (f32[2,128]{1,0:T(2,128)S(1)}, f32[2,128]{1,0:T(2,128)}, u32[]{:S(2)}) copy-start(f32[2,128]{1,0:T(2,128)} %refs_2_.13) | copy-start | bytes 3076
  5.5 0.9 %copy-start.1 = (bf16[2,128,256]{2,1,0:T(8,128)(2,1)S(1)}, bf16[2,128,256]{2,1,0:T(8,128)(2,1)}, u32[]{:S(2)}) copy-start(bf16[2,128,256]{2,1,0:T(8,128)(2,1)} %refs_3_.13) | copy-start | bytes 393220
  6.4 0.9 %copy-start.3 = (bf16[2,256,128]{2,1,0:T(8,128)(2,1)S(1)}, bf16[2,256,128]{2,1,0:T(8,128)(2,1)}, u32[]{:S(2)}) copy-start(bf16[2,256,128]{2,1,0:T(8,128)(2,1)} %refs_4_.13) | copy-start | bytes 393220
  7.3 5.2 %copy-start.2 = (bf16[2,128,256]{2,1,0:T(8,128)(2,1)S(1)}, bf16[2,128,256]{2,1,0:T(8,128)(2,1)}, u32[]{:S(2)}) copy-start(bf16[2,128,256]{2,1,0:T(8,128)(2,1)} %refs_3_.13) | copy-start | bytes 393220
  7.3 12.0 %collective-permute-start.1 = (bf16[4,272,128]{2,1,0:T(8,128)(2,1)S(1)}, bf16[4,272,128]{2,1,0:T(8,128)(2,1)S(1)}, u32[]{:S(2)}, u32[]{:S(2)}) collective-permute-start(bf16[4,272,128]{2,1,0:T(8,128)(2,1)S(1)} %shard_map.64.refs_5_.refs_8_), channel_id=1, source_target_pairs={{0,2},{2,0},{4,6},{6,4},{1,3},{3,1},{5,7},{7,5},{8,10},{10,8},{12,... | collective-permute-start | bytes 835592 | tf_op jit(solution)/shard_map/ppermute | solution.py:219
  11.8 7.5 %collective-permute-start = (bf16[4,272,128]{2,1,0:T(8,128)(2,1)S(1)}, bf16[4,272,128]{2,1,0:T(8,128)(2,1)S(1)}, u32[]{:S(2)}, u32[]{:S(2)}) collective-permute-start(bf16[4,272,128]{2,1,0:T(8,128)(2,1)S(1)} %shard_map.64.refs_5_.refs_8_), channel_id=1, source_target_pairs={{2,4},{4,2},{3,5},{5,3},{10,12},{12,10},{11,13},{13,11},{18,20},{2... | collective-permute-start | bytes 835592 | tf_op jit(solution)/shard_map/ppermute | solution.py:218
  14.1 15.0 %collective-permute-start.9 = (bf16[4,272,128]{2,1,0:T(8,128)(2,1)S(1)}, bf16[4,272,128]{2,1,0:T(8,128)(2,1)S(1)}, u32[]{:S(2)}, u32[]{:S(2)}) collective-permute-start(bf16[4,272,128]{2,1,0:T(8,128)(2,1)S(1)} %get-tuple-element.19.refs_5_.refs_8_.refs_10_), channel_id=1, source_target_pairs={{0,2},{2,0},{4,6},{6,4},{1,3},{3,1},{5,7},{7,5},{8,10},{10,8},{12,... | collective-permute-start | bytes 835592 | tf_op jit(solution)/shard_map/ppermute | solution.py:219
  18.7 11.2 %collective-permute-start.8 = (bf16[4,272,128]{2,1,0:T(8,128)(2,1)S(1)}, bf16[4,272,128]{2,1,0:T(8,128)(2,1)S(1)}, u32[]{:S(2)}, u32[]{:S(2)}) collective-permute-start(bf16[4,272,128]{2,1,0:T(8,128)(2,1)S(1)} %get-tuple-element.19.refs_5_.refs_8_.refs_10_), channel_id=1, source_target_pairs={{2,4},{4,2},{3,5},{5,3},{10,12},{12,10},{11,13},{13,11},{18,20},{2... | collective-permute-start | bytes 835592 | tf_op jit(solution)/shard_map/ppermute | solution.py:218
  20.7 10.6 %collective-permute-start.7 = (bf16[4,224,128]{2,1,0:T(8,128)(2,1)S(1)}, bf16[4,224,128]{2,1,0:T(8,128)(2,1)S(1)}, u32[]{:S(2)}, u32[]{:S(2)}) collective-permute-start(bf16[4,224,128]{2,1,0:T(8,128)(2,1)S(1)} %get-tuple-element.18.refs_5_.refs_8_), channel_id=1, source_target_pairs={{0,2},{2,0},{4,6},{6,4},{1,3},{3,1},{5,7},{7,5},{8,10},{10,8},{12,... | collective-permute-start | bytes 688136 | tf_op jit(solution)/shard_map/ppermute | solution.py:219
  24.5 6.8 %collective-permute-start.6 = (bf16[4,224,128]{2,1,0:T(8,128)(2,1)S(1)}, bf16[4,224,128]{2,1,0:T(8,128)(2,1)S(1)}, u32[]{:S(2)}, u32[]{:S(2)}) collective-permute-start(bf16[4,224,128]{2,1,0:T(8,128)(2,1)S(1)} %get-tuple-element.18.refs_5_.refs_8_), channel_id=1, source_target_pairs={{2,4},{4,2},{3,5},{5,3},{10,12},{12,10},{11,13},{13,11},{18,20},{2... | collective-permute-start | bytes 688136 | tf_op jit(solution)/shard_map/ppermute | solution.py:218
  25.2 4.7 %copy-start.4 = (bf16[2,256,128]{2,1,0:T(8,128)(2,1)S(1)}, bf16[2,256,128]{2,1,0:T(8,128)(2,1)}, u32[]{:S(2)}) copy-start(bf16[2,256,128]{2,1,0:T(8,128)(2,1)} %refs_4_.13) | copy-start | bytes 393220
  25.8 6.8 %collective-permute-start.5 = (bf16[4,80,128]{2,1,0:T(8,128)(2,1)S(1)}, bf16[4,80,128]{2,1,0:T(8,128)(2,1)S(1)}, u32[]{:S(2)}, u32[]{:S(2)}) collective-permute-start(bf16[4,80,128]{2,1,0:T(8,128)(2,1)S(1)} %shard_map.67.refs_5_), channel_id=1, source_target_pairs={{0,2},{2,0},{4,6},{6,4},{1,3},{3,1},{5,7},{7,5},{8,10},{10,8},{12,... | collective-permute-start | bytes 245768 | tf_op jit(solution)/shard_map/ppermute | solution.py:219
  29.1 3.5 %collective-permute-start.4 = (bf16[4,80,128]{2,1,0:T(8,128)(2,1)S(1)}, bf16[4,80,128]{2,1,0:T(8,128)(2,1)S(1)}, u32[]{:S(2)}, u32[]{:S(2)}) collective-permute-start(bf16[4,80,128]{2,1,0:T(8,128)(2,1)S(1)} %shard_map.67.refs_5_), channel_id=1, source_target_pairs={{2,4},{4,2},{3,5},{5,3},{10,12},{12,10},{11,13},{13,11},{18,20},{2... | collective-permute-start | bytes 245768 | tf_op jit(solution)/shard_map/ppermute | solution.py:218

commit v4 on v3

--- a/solution.py
+++ b/solution.py
@@ -15,8 +15,8 @@
 TILE = 32
 
 
-def gelu(x):
-    return 0.5 * x * (1.0 + lax.erf(x * 0.7071067811865476))
+def twice_gelu(x):
+    return x + x * lax.erf(x * 0.7071067811865476)
 
 
 def copy_kernel(lo, state, *refs):
@@ -122,10 +122,10 @@
         var = jnp.mean(centred * centred, axis=-1, keepdims=True)
         normed = (centred * lax.rsqrt(var + 1e-06) * scale).astype(jnp.bfloat16)
         hidden = jnp.dot(normed, w_in[layer], preferred_element_type=jnp.float32)
-        hidden = gelu(hidden).astype(jnp.bfloat16)
+        hidden = twice_gelu(hidden).astype(jnp.bfloat16)
         delta = jnp.dot(hidden, w_out[layer], preferred_element_type=jnp.float32)
         for r in range(rows):
-            new = state[r, pl.ds(at + PAD, tile)].astype(jnp.float32) + delta[r * tile : (r + 1) * tile]
+            new = state[r, pl.ds(at + PAD, tile)].astype(jnp.float32) + 0.5 * delta[r * tile : (r + 1) * tile]
             out[r, pl.ds(at, tile)] = new.astype(jnp.bfloat16)
 
     for at, tile in tiles(made, total, place):

time: 34.4 us -> 34.4 us (level)
  no operation moved by 1% of the time
where the time goes in v4:
time: 34.4 us; the launch traced here: 34.1 us
  starting transfers between devices  22.5 us (65%)
  Pallas kernels  7.82 us (23%)
  local copies, waits for them, and re-layouts  3.53 us (10%)
    ppermute x5, starting transfers between devices, member_step(): even_swap = lax.ppermute(own, 'band', even_pairs)  19.2 us
    pallas_call x6, Pallas kernels, layer_chunk(): pl.pallas_call(functools.partial(chunk_kernel, layer, first, last, offset...  7.8 us
    ppermute x5, starting transfers between devices, member_step(): odd_swap = lax.ppermute(own, 'band', odd_pairs)  3.32 us
    unnamed x16, local copies, waits for them, and re-layouts  2.47 us
    slice x1, local copies, waits for them, and re-layouts, member_step(): chunks = [state[:, :ranges[0][1]]]  1.06 us
  transfers between devices with their start and end apart: 10, of which 0 were waited for; matrix products, arithmetic and copies ran while one was open for 0% of the time, Pallas kernels for 19%

profile of v4, /device:TPU:0, one launch (start us, length us, event | category | flops | bytes accessed | tf_op | source)
XLA Modules:
  0.0 34.1 jit_solution(8535566129647784216)
XLA Ops:
  0.0 1.1 %slice.4.refs_5_.refs_8_.refs_10_ = bf16[4,304,128]{2,1,0:T(8,128)(2,1)S(1)} slice(bf16[4,576,128]{2,1,0:T(8,128)(2,1)} %bitcast.4), slice={[0:4], [0:304], [0:128]} | slice | bytes 622592 | tf_op jit(solution)/shard_map/slice | solution.py:211
  1.1 3.1 %collective-permute-start.3 = (bf16[4,304,128]{2,1,0:T(8,128)(2,1)S(1)}, bf16[4,304,128]{2,1,0:T(8,128)(2,1)S(1)}, u32[]{:S(2)}, u32[]{:S(2)}) collective-permute-start(bf16[4,304,128]{2,1,0:T(8,128)(2,1)S(1)} %slice.4.refs_5_.refs_8_.refs_10_), channel_id=1, source_target_pairs={{0,2},{2,0},{4,6},{6,4},{1,3},{3,1},{5,7},{7,5},{8,10},{10,8},{12,... | collective-permute-start | bytes 933896 | tf_op jit(solution)/shard_map/ppermute | solution.py:219
  4.2 0.7 %collective-permute-start.2 = (bf16[4,304,128]{2,1,0:T(8,128)(2,1)S(1)}, bf16[4,304,128]{2,1,0:T(8,128)(2,1)S(1)}, u32[]{:S(2)}, u32[]{:S(2)}) collective-permute-start(bf16[4,304,128]{2,1,0:T(8,128)(2,1)S(1)} %slice.4.refs_5_.refs_8_.refs_10_), channel_id=1, source_target_pairs={{2,4},{4,2},{3,5},{5,3},{10,12},{12,10},{11,13},{13,11},{18,20},{2... | collective-permute-start | bytes 933896 | tf_op jit(solution)/shard_map/ppermute | solution.py:218
  4.8 0.0 copy-start.7
  4.9 0.6 %copy-done.7 = f32[2,128]{1,0:T(2,128)S(1)} copy-done((f32[2,128]{1,0:T(2,128)S(1)}, f32[2,128]{1,0:T(2,128)}, u32[]{:S(2)}) %copy-start.7) | copy-done | bytes 1048
  5.5 0.9 %copy-done.1 = bf16[2,128,256]{2,1,0:T(8,128)(2,1)S(1)} copy-done((bf16[2,128,256]{2,1,0:T(8,128)(2,1)S(1)}, bf16[2,128,256]{2,1,0:T(8,128)(2,1)}, u32[]{:S(2)}) %copy-start.1) | copy-done | bytes 131096
  6.4 0.9 %copy-done.3 = bf16[2,256,128]{2,1,0:T(8,128)(2,1)S(1)} copy-done((bf16[2,256,128]{2,1,0:T(8,128)(2,1)S(1)}, bf16[2,256,128]{2,1,0:T(8,128)(2,1)}, u32[]{:S(2)}) %copy-start.3) | copy-done | bytes 131096
  7.3 4.4 %collective-permute-start.1 = (bf16[4,272,128]{2,1,0:T(8,128)(2,1)S(1)}, bf16[4,272,128]{2,1,0:T(8,128)(2,1)S(1)}, u32[]{:S(2)}, u32[]{:S(2)}) collective-permute-start(bf16[4,272,128]{2,1,0:T(8,128)(2,1)S(1)} %shard_map.64.refs_5_.refs_8_), channel_id=1, source_target_pairs={{0,2},{2,0},{4,6},{6,4},{1,3},{3,1},{5,7},{7,5},{8,10},{10,8},{12,... | collective-permute-start | bytes 835592 | tf_op jit(solution)/shard_map/ppermute | solution.py:219
  11.8 0.7 %collective-permute-start = (bf16[4,272,128]{2,1,0:T(8,128)(2,1)S(1)}, bf16[4,272,128]{2,1,0:T(8,128)(2,1)S(1)}, u32[]{:S(2)}, u32[]{:S(2)}) collective-permute-start(bf16[4,272,128]{2,1,0:T(8,128)(2,1)S(1)} %shard_map.64.refs_5_.refs_8_), channel_id=1, source_target_pairs={{2,4},{4,2},{3,5},{5,3},{10,12},{12,10},{11,13},{13,11},{18,20},{2... | collective-permute-start | bytes 835592 | tf_op jit(solution)/shard_map/ppermute | solution.py:218
  12.5 0.0 collective-permute-done.2.refs_6_
  12.5 1.6 %shard_map.65 = (bf16[4,272,128]{2,1,0:T(8,128)(2,1)S(1)}, bf16[4,32,128]{2,1,0:T(8,128)(2,1)S(1)}, bf16[4,32,128]{2,1,0:T(8,128)(2,1)S(1)}) custom-call(bf16[9,2,128]{2,1,0:T(2,128)(2,1)S(1)} %bitcast.7, bf16[9,2,128]{2,1,0:T(2,128)(2,1)S(1)} %bitcast.14, f32[2,128]{1,0:T(2,128)S(1)} %copy-done.7, bf16[2,128,256]{2,1,0:T(8,128)(2,1)S(1)} %copy-done.2, ...), custom_call_target="tpu_custom_call" | custom-call | flops 1782579200 | bytes 1114112 | tf_op jit(solution)/shard_map/pallas_call | solution.py:184
  14.1 4.5 %collective-permute-start.9 = (bf16[4,272,128]{2,1,0:T(8,128)(2,1)S(1)}, bf16[4,272,128]{2,1,0:T(8,128)(2,1)S(1)}, u32[]{:S(2)}, u32[]{:S(2)}) collective-permute-start(bf16[4,272,128]{2,1,0:T(8,128)(2,1)S(1)} %get-tuple-element.19.refs_5_.refs_8_.refs_10_), channel_id=1, source_target_pairs={{0,2},{2,0},{4,6},{6,4},{1,3},{3,1},{5,7},{7,5},{8,10},{10,8},{12,... | collective-permute-start | bytes 835592 | tf_op jit(solution)/shard_map/ppermute | solution.py:219
  18.6 0.7 %collective-permute-start.8 = (bf16[4,272,128]{2,1,0:T(8,128)(2,1)S(1)}, bf16[4,272,128]{2,1,0:T(8,128)(2,1)S(1)}, u32[]{:S(2)}, u32[]{:S(2)}) collective-permute-start(bf16[4,272,128]{2,1,0:T(8,128)(2,1)S(1)} %get-tuple-element.19.refs_5_.refs_8_.refs_10_), channel_id=1, source_target_pairs={{2,4},{4,2},{3,5},{5,3},{10,12},{12,10},{11,13},{13,11},{18,20},{2... | collective-permute-start | bytes 835592 | tf_op jit(solution)/shard_map/ppermute | solution.py:218
  19.3 1.3 %shard_map.66 = (bf16[4,224,128]{2,1,0:T(8,128)(2,1)S(1)}, bf16[4,32,128]{2,1,0:T(8,128)(2,1)S(1)}) custom-call(bf16[9,2,128]{2,1,0:T(2,128)(2,1)S(1)} %bitcast.8, bf16[9,2,128]{2,1,0:T(2,128)(2,1)S(1)} %bitcast.15, f32[2,128]{1,0:T(2,128)S(1)} %copy-done.7, bf16[2,128,256]{2,1,0:T(8,128)(2,1)S(1)} %copy-done.2, bf16[2,256,128]{2,1,0:T(8,128)(2,1)S(1)} %copy-done.3, ...), custom_call_target="tpu_custom_call" | custom-call | flops 1468006400 | bytes 917504 | tf_op jit(solution)/shard_map/pallas_call | solution.py:184
  20.6 3.8 %collective-permute-start.7 = (bf16[4,224,128]{2,1,0:T(8,128)(2,1)S(1)}, bf16[4,224,128]{2,1,0:T(8,128)(2,1)S(1)}, u32[]{:S(2)}, u32[]{:S(2)}) collective-permute-start(bf16[4,224,128]{2,1,0:T(8,128)(2,1)S(1)} %get-tuple-element.18.refs_5_.refs_8_), channel_id=1, source_target_pairs={{0,2},{2,0},{4,6},{6,4},{1,3},{3,1},{5,7},{7,5},{8,10},{10,8},{12,... | collective-permute-start | bytes 688136 | tf_op jit(solution)/shard_map/ppermute | solution.py:219
  24.5 0.7 %collective-permute-start.6 = (bf16[4,224,128]{2,1,0:T(8,128)(2,1)S(1)}, bf16[4,224,128]{2,1,0:T(8,128)(2,1)S(1)}, u32[]{:S(2)}, u32[]{:S(2)}) collective-permute-start(bf16[4,224,128]{2,1,0:T(8,128)(2,1)S(1)} %get-tuple-element.18.refs_5_.refs_8_), channel_id=1, source_target_pairs={{2,4},{4,2},{3,5},{5,3},{10,12},{12,10},{11,13},{13,11},{18,20},{2... | collective-permute-start | bytes 688136 | tf_op jit(solution)/shard_map/ppermute | solution.py:218
  25.1 0.0 copy-start.4
  25.1 0.7 %shard_map.67.refs_5_ = bf16[4,80,128]{2,1,0:T(8,128)(2,1)S(1)} custom-call(bf16[9,2,128]{2,1,0:T(2,128)(2,1)S(1)} %bitcast.9, bf16[9,2,128]{2,1,0:T(2,128)(2,1)S(1)} %bitcast.16, f32[2,128]{1,0:T(2,128)S(1)} %copy-done.7, bf16[2,128,256]{2,1,0:T(8,128)(2,1)S(1)} %copy-done.2, bf16[2,256,128]{2,1,0:T(8,128)(2,1)S(1)} %copy-done.3, ...), custom_call_target="tpu_custom_call" | custom-call | flops 524288000 | bytes 327680 | tf_op jit(solution)/shard_map/pallas_call | solution.py:184
  25.8 3.3 %collective-permute-start.5 = (bf16[4,80,128]{2,1,0:T(8,128)(2,1)S(1)}, bf16[4,80,128]{2,1,0:T(8,128)(2,1)S(1)}, u32[]{:S(2)}, u32[]{:S(2)}) collective-permute-start(bf16[4,80,128]{2,1,0:T(8,128)(2,1)S(1)} %shard_map.67.refs_5_), channel_id=1, source_target_pairs={{0,2},{2,0},{4,6},{6,4},{1,3},{3,1},{5,7},{7,5},{8,10},{10,8},{12,... | collective-permute-start | bytes 245768 | tf_op jit(solution)/shard_map/ppermute | solution.py:219
  29.1 0.7 %collective-permute-start.4 = (bf16[4,80,128]{2,1,0:T(8,128)(2,1)S(1)}, bf16[4,80,128]{2,1,0:T(8,128)(2,1)S(1)}, u32[]{:S(2)}, u32[]{:S(2)}) collective-permute-start(bf16[4,80,128]{2,1,0:T(8,128)(2,1)S(1)} %shard_map.67.refs_5_), channel_id=1, source_target_pairs={{2,4},{4,2},{3,5},{5,3},{10,12},{12,10},{11,13},{13,11},{18,20},{2... | collective-permute-start | bytes 245768 | tf_op jit(solution)/shard_map/ppermute | solution.py:218
  29.8 1.4 %shard_map.68 = (bf16[4,240,128]{2,1,0:T(8,128)(2,1)S(1)}, bf16[4,32,128]{2,1,0:T(8,128)(2,1)S(1)}, bf16[4,32,128]{2,1,0:T(8,128)(2,1)S(1)}) custom-call(bf16[9,2,128]{2,1,0:T(2,128)(2,1)S(1)} %bitcast.10, bf16[9,2,128]{2,1,0:T(2,128)(2,1)S(1)} %bitcast.17, f32[2,128]{1,0:T(2,128)S(1)} %copy-done.7, bf16[2,128,256]{2,1,0:T(8,128)(2,1)S(1)} %copy-done.2, ...), custom_call_target="tpu_custom_call" | custom-call | flops 1572864000 | bytes 983040 | tf_op jit(solution)/shard_map/pallas_call | solution.py:184
  31.3 0.0 collective-permute-done.6.refs_6_
  31.3 1.3 %shard_map.69 = (bf16[4,224,128]{2,1,0:T(8,128)(2,1)S(1)}, bf16[4,32,128]{2,1,0:T(8,128)(2,1)S(1)}) custom-call(bf16[9,2,128]{2,1,0:T(2,128)(2,1)S(1)} %bitcast.11, bf16[9,2,128]{2,1,0:T(2,128)(2,1)S(1)} %bitcast.18, f32[2,128]{1,0:T(2,128)S(1)} %copy-done.7, bf16[2,128,256]{2,1,0:T(8,128)(2,1)S(1)} %copy-done.2, bf16[2,256,128]{2,1,0:T(8,128)(2,1)S(1)} %copy-done.4, ...), custom_call_target="tpu_custom_call" | custom-call | flops 1468006400 | bytes 917504 | tf_op jit(solution)/shard_map/pallas_call | solution.py:184
  32.6 1.5 %shard_map.70 = bf16[4,576,128]{2,1,0:T(8,128)(2,1)} custom-call(bf16[9,2,128]{2,1,0:T(2,128)(2,1)S(1)} %bitcast.12, bf16[9,2,128]{2,1,0:T(2,128)(2,1)S(1)} %bitcast.19, f32[2,128]{1,0:T(2,128)S(1)} %copy-done.7, bf16[2,128,256]{2,1,0:T(8,128)(2,1)S(1)} %copy-done.2, bf16[2,256,128]{2,1,0:T(8,128)(2,1)S(1)} %copy-done.4, ...), custom_call_target="tpu_custom_call" | custom-call | flops 734003200 | bytes 458752 | tf_op jit(solution)/shard_map/pallas_call | solution.py:184
  (20 shorter events, 0.1 us)
Async XLA Ops:
  0.0 4.8 %copy-start = (bf16[1,4,576,128]{3,2,1,0:T(8,128)(2,1)S(1)}, bf16[1,4,576,128]{3,2,1,0:T(8,128)(2,1)}, u32[]{:S(2)}) copy-start(bf16[1,4,576,128]{3,2,1,0:T(8,128)(2,1)} %param.6) | copy-start | bytes 1769476
  0.0 4.9 %copy-start.5 = (bf16[2,9,128]{2,0,1:T(2,128)(2,1)S(1)}, bf16[2,9,128]{2,0,1:T(2,128)(2,1)}, u32[]{:S(2)}) copy-start(bf16[2,9,128]{2,0,1:T(2,128)(2,1)} %param.7) | copy-start | bytes 13828
  0.0 4.9 %copy-start.6 = (bf16[2,9,128]{2,0,1:T(2,128)(2,1)S(1)}, bf16[2,9,128]{2,0,1:T(2,128)(2,1)}, u32[]{:S(2)}) copy-start(bf16[2,9,128]{2,0,1:T(2,128)(2,1)} %param.8) | copy-start | bytes 13828
  1.1 11.4 %collective-permute-start.3 = (bf16[4,304,128]{2,1,0:T(8,128)(2,1)S(1)}, bf16[4,304,128]{2,1,0:T(8,128)(2,1)S(1)}, u32[]{:S(2)}, u32[]{:S(2)}) collective-permute-start(bf16[4,304,128]{2,1,0:T(8,128)(2,1)S(1)} %slice.4.refs_5_.refs_8_.refs_10_), channel_id=1, source_target_pairs={{0,2},{2,0},{4,6},{6,4},{1,3},{3,1},{5,7},{7,5},{8,10},{10,8},{12,... | collective-permute-start | bytes 933896 | tf_op jit(solution)/shard_map/ppermute | solution.py:219
  4.2 8.3 %collective-permute-start.2 = (bf16[4,304,128]{2,1,0:T(8,128)(2,1)S(1)}, bf16[4,304,128]{2,1,0:T(8,128)(2,1)S(1)}, u32[]{:S(2)}, u32[]{:S(2)}) collective-permute-start(bf16[4,304,128]{2,1,0:T(8,128)(2,1)S(1)} %slice.4.refs_5_.refs_8_.refs_10_), channel_id=1, source_target_pairs={{2,4},{4,2},{3,5},{5,3},{10,12},{12,10},{11,13},{13,11},{18,20},{2... | collective-permute-start | bytes 933896 | tf_op jit(solution)/shard_map/ppermute | solution.py:218
  4.8 0.7 %copy-start.7 = (f32[2,128]{1,0:T(2,128)S(1)}, f32[2,128]{1,0:T(2,128)}, u32[]{:S(2)}) copy-start(f32[2,128]{1,0:T(2,128)} %refs_2_.13) | copy-start | bytes 3076
  5.5 0.9 %copy-start.1 = (bf16[2,128,256]{2,1,0:T(8,128)(2,1)S(1)}, bf16[2,128,256]{2,1,0:T(8,128)(2,1)}, u32[]{:S(2)}) copy-start(bf16[2,128,256]{2,1,0:T(8,128)(2,1)} %refs_3_.13) | copy-start | bytes 393220
  6.4 0.9 %copy-start.3 = (bf16[2,256,128]{2,1,0:T(8,128)(2,1)S(1)}, bf16[2,256,128]{2,1,0:T(8,128)(2,1)}, u32[]{:S(2)}) copy-start(bf16[2,256,128]{2,1,0:T(8,128)(2,1)} %refs_4_.13) | copy-start | bytes 393220
  7.3 5.2 %copy-start.2 = (bf16[2,128,256]{2,1,0:T(8,128)(2,1)S(1)}, bf16[2,128,256]{2,1,0:T(8,128)(2,1)}, u32[]{:S(2)}) copy-start(bf16[2,128,256]{2,1,0:T(8,128)(2,1)} %refs_3_.13) | copy-start | bytes 393220
  7.3 12.0 %collective-permute-start.1 = (bf16[4,272,128]{2,1,0:T(8,128)(2,1)S(1)}, bf16[4,272,128]{2,1,0:T(8,128)(2,1)S(1)}, u32[]{:S(2)}, u32[]{:S(2)}) collective-permute-start(bf16[4,272,128]{2,1,0:T(8,128)(2,1)S(1)} %shard_map.64.refs_5_.refs_8_), channel_id=1, source_target_pairs={{0,2},{2,0},{4,6},{6,4},{1,3},{3,1},{5,7},{7,5},{8,10},{10,8},{12,... | collective-permute-start | bytes 835592 | tf_op jit(solution)/shard_map/ppermute | solution.py:219
  11.8 7.5 %collective-permute-start = (bf16[4,272,128]{2,1,0:T(8,128)(2,1)S(1)}, bf16[4,272,128]{2,1,0:T(8,128)(2,1)S(1)}, u32[]{:S(2)}, u32[]{:S(2)}) collective-permute-start(bf16[4,272,128]{2,1,0:T(8,128)(2,1)S(1)} %shard_map.64.refs_5_.refs_8_), channel_id=1, source_target_pairs={{2,4},{4,2},{3,5},{5,3},{10,12},{12,10},{11,13},{13,11},{18,20},{2... | collective-permute-start | bytes 835592 | tf_op jit(solution)/shard_map/ppermute | solution.py:218
  14.1 15.0 %collective-permute-start.9 = (bf16[4,272,128]{2,1,0:T(8,128)(2,1)S(1)}, bf16[4,272,128]{2,1,0:T(8,128)(2,1)S(1)}, u32[]{:S(2)}, u32[]{:S(2)}) collective-permute-start(bf16[4,272,128]{2,1,0:T(8,128)(2,1)S(1)} %get-tuple-element.19.refs_5_.refs_8_.refs_10_), channel_id=1, source_target_pairs={{0,2},{2,0},{4,6},{6,4},{1,3},{3,1},{5,7},{7,5},{8,10},{10,8},{12,... | collective-permute-start | bytes 835592 | tf_op jit(solution)/shard_map/ppermute | solution.py:219
  18.6 11.2 %collective-permute-start.8 = (bf16[4,272,128]{2,1,0:T(8,128)(2,1)S(1)}, bf16[4,272,128]{2,1,0:T(8,128)(2,1)S(1)}, u32[]{:S(2)}, u32[]{:S(2)}) collective-permute-start(bf16[4,272,128]{2,1,0:T(8,128)(2,1)S(1)} %get-tuple-element.19.refs_5_.refs_8_.refs_10_), channel_id=1, source_target_pairs={{2,4},{4,2},{3,5},{5,3},{10,12},{12,10},{11,13},{13,11},{18,20},{2... | collective-permute-start | bytes 835592 | tf_op jit(solution)/shard_map/ppermute | solution.py:218
  20.6 10.6 %collective-permute-start.7 = (bf16[4,224,128]{2,1,0:T(8,128)(2,1)S(1)}, bf16[4,224,128]{2,1,0:T(8,128)(2,1)S(1)}, u32[]{:S(2)}, u32[]{:S(2)}) collective-permute-start(bf16[4,224,128]{2,1,0:T(8,128)(2,1)S(1)} %get-tuple-element.18.refs_5_.refs_8_), channel_id=1, source_target_pairs={{0,2},{2,0},{4,6},{6,4},{1,3},{3,1},{5,7},{7,5},{8,10},{10,8},{12,... | collective-permute-start | bytes 688136 | tf_op jit(solution)/shard_map/ppermute | solution.py:219
  24.5 6.8 %collective-permute-start.6 = (bf16[4,224,128]{2,1,0:T(8,128)(2,1)S(1)}, bf16[4,224,128]{2,1,0:T(8,128)(2,1)S(1)}, u32[]{:S(2)}, u32[]{:S(2)}) collective-permute-start(bf16[4,224,128]{2,1,0:T(8,128)(2,1)S(1)} %get-tuple-element.18.refs_5_.refs_8_), channel_id=1, source_target_pairs={{2,4},{4,2},{3,5},{5,3},{10,12},{12,10},{11,13},{13,11},{18,20},{2... | collective-permute-start | bytes 688136 | tf_op jit(solution)/shard_map/ppermute | solution.py:218
  25.1 4.7 %copy-start.4 = (bf16[2,256,128]{2,1,0:T(8,128)(2,1)S(1)}, bf16[2,256,128]{2,1,0:T(8,128)(2,1)}, u32[]{:S(2)}) copy-start(bf16[2,256,128]{2,1,0:T(8,128)(2,1)} %refs_4_.13) | copy-start | bytes 393220
  25.8 6.8 %collective-permute-start.5 = (bf16[4,80,128]{2,1,0:T(8,128)(2,1)S(1)}, bf16[4,80,128]{2,1,0:T(8,128)(2,1)S(1)}, u32[]{:S(2)}, u32[]{:S(2)}) collective-permute-start(bf16[4,80,128]{2,1,0:T(8,128)(2,1)S(1)} %shard_map.67.refs_5_), channel_id=1, source_target_pairs={{0,2},{2,0},{4,6},{6,4},{1,3},{3,1},{5,7},{7,5},{8,10},{10,8},{12,... | collective-permute-start | bytes 245768 | tf_op jit(solution)/shard_map/ppermute | solution.py:219
  29.1 3.5 %collective-permute-start.4 = (bf16[4,80,128]{2,1,0:T(8,128)(2,1)S(1)}, bf16[4,80,128]{2,1,0:T(8,128)(2,1)S(1)}, u32[]{:S(2)}, u32[]{:S(2)}) collective-permute-start(bf16[4,80,128]{2,1,0:T(8,128)(2,1)S(1)} %shard_map.67.refs_5_), channel_id=1, source_target_pairs={{2,4},{4,2},{3,5},{5,3},{10,12},{12,10},{11,13},{13,11},{18,20},{2... | collective-permute-start | bytes 245768 | tf_op jit(solution)/shard_map/ppermute | solution.py:218

commit v5 on v3

--- a/solution.py
+++ b/solution.py
@@ -210,7 +210,7 @@
     ranges = splits(lons)
     chunks = [state[:, : ranges[0][1]]]
     for lo, hi in ranges[1:]:
-        chunks.append(later_columns(state, lo, hi, weights))
+        chunks.append(later_columns(state, lo, hi, weights[:4]))
     place, earlier = LAYERS * PAD, []
     for layer in range(LAYERS):
         halos = []

time: 34.4 us -> 34.4 us (level)
  local copies, waits for them, and re-layouts: 3.53 us -> 2.62 us
  starting transfers between devices: 22.5 us -> 23.1 us
  waiting for transfers between devices: 0.03 us -> 0.4 us
    unnamed x16 -> x14, local copies, waits for them, and re-layouts: 2.47 us -> 1.57 us
    ppermute x5, starting transfers between devices: 19.2 us -> 19.7 us  [member_step(): even_swap = lax.ppermute(own, 'band', even_pairs)]
    ppermute x5, waiting for transfers between devices: 0.01 us -> 0.39 us  [member_step(): even_swap = lax.ppermute(own, 'band', even_pairs)]
  transfers between devices with their start and end apart: 10 -> 10, of which waited for: 0 -> 1; matrix products, arithmetic and copies ran while one was open for 0% -> 0% of each run, Pallas kernels for 19% -> 19%
where the time goes in v5:
time: 34.4 us; the launch traced here: 34.1 us
  starting transfers between devices  23.1 us (67%)
  Pallas kernels  7.86 us (23%)
  local copies, waits for them, and re-layouts  2.62 us (8%)
  waiting for transfers between devices  0.4 us (1%)
    ppermute x5, starting transfers between devices, member_step(): even_swap = lax.ppermute(own, 'band', even_pairs)  19.7 us
    pallas_call x6, Pallas kernels, layer_chunk(): pl.pallas_call(functools.partial(chunk_kernel, layer, first, last, offset...  7.84 us
    ppermute x5, starting transfers between devices, member_step(): odd_swap = lax.ppermute(own, 'band', odd_pairs)  3.32 us
    unnamed x14, local copies, waits for them, and re-layouts  1.57 us
    slice x1, local copies, waits for them, and re-layouts, member_step(): chunks = [state[:, :ranges[0][1]]]  1.06 us
  transfers between devices with their start and end apart: 10, of which 1 were waited for; matrix products, arithmetic and copies ran while one was open for 0% of the time, Pallas kernels for 19%

profile of v5, /device:TPU:0, one launch (start us, length us, event | category | flops | bytes accessed | tf_op | source)
XLA Modules:
  0.0 34.1 jit_solution(7996243427807046880)
XLA Ops:
  0.0 1.1 %slice.4.refs_5_.refs_8_.refs_10_ = bf16[4,304,128]{2,1,0:T(8,128)(2,1)S(1)} slice(bf16[4,576,128]{2,1,0:T(8,128)(2,1)} %bitcast.4), slice={[0:4], [0:304], [0:128]} | slice | bytes 622592 | tf_op jit(solution)/shard_map/slice | solution.py:211
  1.1 3.1 %collective-permute-start.3 = (bf16[4,304,128]{2,1,0:T(8,128)(2,1)S(1)}, bf16[4,304,128]{2,1,0:T(8,128)(2,1)S(1)}, u32[]{:S(2)}, u32[]{:S(2)}) collective-permute-start(bf16[4,304,128]{2,1,0:T(8,128)(2,1)S(1)} %slice.4.refs_5_.refs_8_.refs_10_), channel_id=1, source_target_pairs={{0,2},{2,0},{4,6},{6,4},{1,3},{3,1},{5,7},{7,5},{8,10},{10,8},{12,... | collective-permute-start | bytes 933896 | tf_op jit(solution)/shard_map/ppermute | solution.py:219
  4.2 0.7 %collective-permute-start.2 = (bf16[4,304,128]{2,1,0:T(8,128)(2,1)S(1)}, bf16[4,304,128]{2,1,0:T(8,128)(2,1)S(1)}, u32[]{:S(2)}, u32[]{:S(2)}) collective-permute-start(bf16[4,304,128]{2,1,0:T(8,128)(2,1)S(1)} %slice.4.refs_5_.refs_8_.refs_10_), channel_id=1, source_target_pairs={{2,4},{4,2},{3,5},{5,3},{10,12},{12,10},{11,13},{13,11},{18,20},{2... | collective-permute-start | bytes 933896 | tf_op jit(solution)/shard_map/ppermute | solution.py:218
  4.8 0.0 copy-start.6
  4.9 0.6 %copy-done.6 = f32[2,128]{1,0:T(2,128)S(1)} copy-done((f32[2,128]{1,0:T(2,128)S(1)}, f32[2,128]{1,0:T(2,128)}, u32[]{:S(2)}) %copy-start.6) | copy-done | bytes 1048
  5.5 0.9 %copy-done.1 = bf16[2,128,256]{2,1,0:T(8,128)(2,1)S(1)} copy-done((bf16[2,128,256]{2,1,0:T(8,128)(2,1)S(1)}, bf16[2,128,256]{2,1,0:T(8,128)(2,1)}, u32[]{:S(2)}) %copy-start.1) | copy-done | bytes 131096
  6.4 4.4 %collective-permute-start.1 = (bf16[4,272,128]{2,1,0:T(8,128)(2,1)S(1)}, bf16[4,272,128]{2,1,0:T(8,128)(2,1)S(1)}, u32[]{:S(2)}, u32[]{:S(2)}) collective-permute-start(bf16[4,272,128]{2,1,0:T(8,128)(2,1)S(1)} %shard_map.64.refs_5_.refs_8_), channel_id=1, source_target_pairs={{0,2},{2,0},{4,6},{6,4},{1,3},{3,1},{5,7},{7,5},{8,10},{10,8},{12,... | collective-permute-start | bytes 835592 | tf_op jit(solution)/shard_map/ppermute | solution.py:219
  10.9 0.7 %collective-permute-start = (bf16[4,272,128]{2,1,0:T(8,128)(2,1)S(1)}, bf16[4,272,128]{2,1,0:T(8,128)(2,1)S(1)}, u32[]{:S(2)}, u32[]{:S(2)}) collective-permute-start(bf16[4,272,128]{2,1,0:T(8,128)(2,1)S(1)} %shard_map.64.refs_5_.refs_8_), channel_id=1, source_target_pairs={{2,4},{4,2},{3,5},{5,3},{10,12},{12,10},{11,13},{13,11},{18,20},{2... | collective-permute-start | bytes 835592 | tf_op jit(solution)/shard_map/ppermute | solution.py:218
  11.6 0.4 %collective-permute-done.3.refs_7_ = bf16[4,304,128]{2,1,0:T(8,128)(2,1)S(1)} collective-permute-done((bf16[4,304,128]{2,1,0:T(8,128)(2,1)S(1)}, bf16[4,304,128]{2,1,0:T(8,128)(2,1)S(1)}, u32[]{:S(2)}, u32[]{:S(2)}) %collective-permute-start.3) | collective-permute-done | bytes 311328 | tf_op jit(solution)/shard_map/ppermute | solution.py:219
  11.9 1.6 %shard_map.65 = (bf16[4,272,128]{2,1,0:T(8,128)(2,1)S(1)}, bf16[4,32,128]{2,1,0:T(8,128)(2,1)S(1)}, bf16[4,32,128]{2,1,0:T(8,128)(2,1)S(1)}) custom-call(bf16[9,2,128]{2,1,0:T(2,128)(2,1)S(1)} %bitcast.7, bf16[9,2,128]{2,1,0:T(2,128)(2,1)S(1)} %bitcast.14, f32[2,128]{1,0:T(2,128)S(1)} %copy-done.6, bf16[2,128,256]{2,1,0:T(8,128)(2,1)S(1)} %copy-done.1, ...), custom_call_target="tpu_custom_call" | custom-call | flops 1782579200 | bytes 1114112 | tf_op jit(solution)/shard_map/pallas_call | solution.py:184
  13.6 5.5 %collective-permute-start.9 = (bf16[4,272,128]{2,1,0:T(8,128)(2,1)S(1)}, bf16[4,272,128]{2,1,0:T(8,128)(2,1)S(1)}, u32[]{:S(2)}, u32[]{:S(2)}) collective-permute-start(bf16[4,272,128]{2,1,0:T(8,128)(2,1)S(1)} %get-tuple-element.19.refs_5_.refs_8_.refs_10_), channel_id=1, source_target_pairs={{0,2},{2,0},{4,6},{6,4},{1,3},{3,1},{5,7},{7,5},{8,10},{10,8},{12,... | collective-permute-start | bytes 835592 | tf_op jit(solution)/shard_map/ppermute | solution.py:219
  19.1 0.7 %collective-permute-start.8 = (bf16[4,272,128]{2,1,0:T(8,128)(2,1)S(1)}, bf16[4,272,128]{2,1,0:T(8,128)(2,1)S(1)}, u32[]{:S(2)}, u32[]{:S(2)}) collective-permute-start(bf16[4,272,128]{2,1,0:T(8,128)(2,1)S(1)} %get-tuple-element.19.refs_5_.refs_8_.refs_10_), channel_id=1, source_target_pairs={{2,4},{4,2},{3,5},{5,3},{10,12},{12,10},{11,13},{13,11},{18,20},{2... | collective-permute-start | bytes 835592 | tf_op jit(solution)/shard_map/ppermute | solution.py:218
  19.8 0.0 collective-permute-done.1.refs_7_
  19.8 1.3 %shard_map.66 = (bf16[4,224,128]{2,1,0:T(8,128)(2,1)S(1)}, bf16[4,32,128]{2,1,0:T(8,128)(2,1)S(1)}) custom-call(bf16[9,2,128]{2,1,0:T(2,128)(2,1)S(1)} %bitcast.8, bf16[9,2,128]{2,1,0:T(2,128)(2,1)S(1)} %bitcast.15, f32[2,128]{1,0:T(2,128)S(1)} %copy-done.6, bf16[2,128,256]{2,1,0:T(8,128)(2,1)S(1)} %copy-done.1, bf16[2,256,128]{2,1,0:T(8,128)(2,1)S(1)} %copy-done.3, ...), custom_call_target="tpu_custom_call" | custom-call | flops 1468006400 | bytes 917504 | tf_op jit(solution)/shard_map/pallas_call | solution.py:184
  21.1 3.4 %collective-permute-start.7 = (bf16[4,224,128]{2,1,0:T(8,128)(2,1)S(1)}, bf16[4,224,128]{2,1,0:T(8,128)(2,1)S(1)}, u32[]{:S(2)}, u32[]{:S(2)}) collective-permute-start(bf16[4,224,128]{2,1,0:T(8,128)(2,1)S(1)} %get-tuple-element.18.refs_5_.refs_8_), channel_id=1, source_target_pairs={{0,2},{2,0},{4,6},{6,4},{1,3},{3,1},{5,7},{7,5},{8,10},{10,8},{12,... | collective-permute-start | bytes 688136 | tf_op jit(solution)/shard_map/ppermute | solution.py:219
  24.5 0.7 %collective-permute-start.6 = (bf16[4,224,128]{2,1,0:T(8,128)(2,1)S(1)}, bf16[4,224,128]{2,1,0:T(8,128)(2,1)S(1)}, u32[]{:S(2)}, u32[]{:S(2)}) collective-permute-start(bf16[4,224,128]{2,1,0:T(8,128)(2,1)S(1)} %get-tuple-element.18.refs_5_.refs_8_), channel_id=1, source_target_pairs={{2,4},{4,2},{3,5},{5,3},{10,12},{12,10},{11,13},{13,11},{18,20},{2... | collective-permute-start | bytes 688136 | tf_op jit(solution)/shard_map/ppermute | solution.py:218
  25.2 0.0 copy-start.2
  25.2 0.7 %shard_map.67.refs_5_ = bf16[4,80,128]{2,1,0:T(8,128)(2,1)S(1)} custom-call(bf16[9,2,128]{2,1,0:T(2,128)(2,1)S(1)} %bitcast.9, bf16[9,2,128]{2,1,0:T(2,128)(2,1)S(1)} %bitcast.16, f32[2,128]{1,0:T(2,128)S(1)} %copy-done.6, bf16[2,128,256]{2,1,0:T(8,128)(2,1)S(1)} %copy-done.1, bf16[2,256,128]{2,1,0:T(8,128)(2,1)S(1)} %copy-done.3, ...), custom_call_target="tpu_custom_call" | custom-call | flops 524288000 | bytes 327680 | tf_op jit(solution)/shard_map/pallas_call | solution.py:184
  25.8 3.3 %collective-permute-start.5 = (bf16[4,80,128]{2,1,0:T(8,128)(2,1)S(1)}, bf16[4,80,128]{2,1,0:T(8,128)(2,1)S(1)}, u32[]{:S(2)}, u32[]{:S(2)}) collective-permute-start(bf16[4,80,128]{2,1,0:T(8,128)(2,1)S(1)} %shard_map.67.refs_5_), channel_id=1, source_target_pairs={{0,2},{2,0},{4,6},{6,4},{1,3},{3,1},{5,7},{7,5},{8,10},{10,8},{12,... | collective-permute-start | bytes 245768 | tf_op jit(solution)/shard_map/ppermute | solution.py:219
  29.1 0.7 %collective-permute-start.4 = (bf16[4,80,128]{2,1,0:T(8,128)(2,1)S(1)}, bf16[4,80,128]{2,1,0:T(8,128)(2,1)S(1)}, u32[]{:S(2)}, u32[]{:S(2)}) collective-permute-start(bf16[4,80,128]{2,1,0:T(8,128)(2,1)S(1)} %shard_map.67.refs_5_), channel_id=1, source_target_pairs={{2,4},{4,2},{3,5},{5,3},{10,12},{12,10},{11,13},{13,11},{18,20},{2... | collective-permute-start | bytes 245768 | tf_op jit(solution)/shard_map/ppermute | solution.py:218
  29.8 1.5 %shard_map.68 = (bf16[4,240,128]{2,1,0:T(8,128)(2,1)S(1)}, bf16[4,32,128]{2,1,0:T(8,128)(2,1)S(1)}, bf16[4,32,128]{2,1,0:T(8,128)(2,1)S(1)}) custom-call(bf16[9,2,128]{2,1,0:T(2,128)(2,1)S(1)} %bitcast.10, bf16[9,2,128]{2,1,0:T(2,128)(2,1)S(1)} %bitcast.17, f32[2,128]{1,0:T(2,128)S(1)} %copy-done.6, bf16[2,128,256]{2,1,0:T(8,128)(2,1)S(1)} %copy-done.2, ...), custom_call_target="tpu_custom_call" | custom-call | flops 1572864000 | bytes 983040 | tf_op jit(solution)/shard_map/pallas_call | solution.py:184
  31.3 0.0 collective-permute-done.6.refs_6_
  31.3 1.3 %shard_map.69 = (bf16[4,224,128]{2,1,0:T(8,128)(2,1)S(1)}, bf16[4,32,128]{2,1,0:T(8,128)(2,1)S(1)}) custom-call(bf16[9,2,128]{2,1,0:T(2,128)(2,1)S(1)} %bitcast.11, bf16[9,2,128]{2,1,0:T(2,128)(2,1)S(1)} %bitcast.18, f32[2,128]{1,0:T(2,128)S(1)} %copy-done.6, bf16[2,128,256]{2,1,0:T(8,128)(2,1)S(1)} %copy-done.2, bf16[2,256,128]{2,1,0:T(8,128)(2,1)S(1)} %copy-done.3, ...), custom_call_target="tpu_custom_call" | custom-call | flops 1468006400 | bytes 917504 | tf_op jit(solution)/shard_map/pallas_call | solution.py:184
  32.6 1.5 %shard_map.70 = bf16[4,576,128]{2,1,0:T(8,128)(2,1)} custom-call(bf16[9,2,128]{2,1,0:T(2,128)(2,1)S(1)} %bitcast.12, bf16[9,2,128]{2,1,0:T(2,128)(2,1)S(1)} %bitcast.19, f32[2,128]{1,0:T(2,128)S(1)} %copy-done.6, bf16[2,128,256]{2,1,0:T(8,128)(2,1)S(1)} %copy-done.2, bf16[2,256,128]{2,1,0:T(8,128)(2,1)S(1)} %copy-done.3, ...), custom_call_target="tpu_custom_call" | custom-call | flops 734003200 | bytes 458752 | tf_op jit(solution)/shard_map/pallas_call | solution.py:184
  (18 shorter events, 0.1 us)
Async XLA Ops:
  0.0 4.8 %copy-start = (bf16[1,4,576,128]{3,2,1,0:T(8,128)(2,1)S(1)}, bf16[1,4,576,128]{3,2,1,0:T(8,128)(2,1)}, u32[]{:S(2)}) copy-start(bf16[1,4,576,128]{3,2,1,0:T(8,128)(2,1)} %param.6) | copy-start | bytes 1769476
  0.0 4.9 %copy-start.4 = (bf16[2,9,128]{2,0,1:T(2,128)(2,1)S(1)}, bf16[2,9,128]{2,0,1:T(2,128)(2,1)}, u32[]{:S(2)}) copy-start(bf16[2,9,128]{2,0,1:T(2,128)(2,1)} %param.7) | copy-start | bytes 13828
  0.0 4.9 %copy-start.5 = (bf16[2,9,128]{2,0,1:T(2,128)(2,1)S(1)}, bf16[2,9,128]{2,0,1:T(2,128)(2,1)}, u32[]{:S(2)}) copy-start(bf16[2,9,128]{2,0,1:T(2,128)(2,1)} %param.8) | copy-start | bytes 13828
  1.1 10.9 %collective-permute-start.3 = (bf16[4,304,128]{2,1,0:T(8,128)(2,1)S(1)}, bf16[4,304,128]{2,1,0:T(8,128)(2,1)S(1)}, u32[]{:S(2)}, u32[]{:S(2)}) collective-permute-start(bf16[4,304,128]{2,1,0:T(8,128)(2,1)S(1)} %slice.4.refs_5_.refs_8_.refs_10_), channel_id=1, source_target_pairs={{0,2},{2,0},{4,6},{6,4},{1,3},{3,1},{5,7},{7,5},{8,10},{10,8},{12,... | collective-permute-start | bytes 933896 | tf_op jit(solution)/shard_map/ppermute | solution.py:219
  4.2 7.8 %collective-permute-start.2 = (bf16[4,304,128]{2,1,0:T(8,128)(2,1)S(1)}, bf16[4,304,128]{2,1,0:T(8,128)(2,1)S(1)}, u32[]{:S(2)}, u32[]{:S(2)}) collective-permute-start(bf16[4,304,128]{2,1,0:T(8,128)(2,1)S(1)} %slice.4.refs_5_.refs_8_.refs_10_), channel_id=1, source_target_pairs={{2,4},{4,2},{3,5},{5,3},{10,12},{12,10},{11,13},{13,11},{18,20},{2... | collective-permute-start | bytes 933896 | tf_op jit(solution)/shard_map/ppermute | solution.py:218
  4.8 0.7 %copy-start.6 = (f32[2,128]{1,0:T(2,128)S(1)}, f32[2,128]{1,0:T(2,128)}, u32[]{:S(2)}) copy-start(f32[2,128]{1,0:T(2,128)} %refs_2_.13) | copy-start | bytes 3076
  5.5 0.9 %copy-start.1 = (bf16[2,128,256]{2,1,0:T(8,128)(2,1)S(1)}, bf16[2,128,256]{2,1,0:T(8,128)(2,1)}, u32[]{:S(2)}) copy-start(bf16[2,128,256]{2,1,0:T(8,128)(2,1)} %refs_3_.13) | copy-start | bytes 393220
  6.4 5.5 %copy-start.3 = (bf16[2,256,128]{2,1,0:T(8,128)(2,1)S(1)}, bf16[2,256,128]{2,1,0:T(8,128)(2,1)}, u32[]{:S(2)}) copy-start(bf16[2,256,128]{2,1,0:T(8,128)(2,1)} %refs_4_.11) | copy-start | bytes 393220
  6.4 13.3 %collective-permute-start.1 = (bf16[4,272,128]{2,1,0:T(8,128)(2,1)S(1)}, bf16[4,272,128]{2,1,0:T(8,128)(2,1)S(1)}, u32[]{:S(2)}, u32[]{:S(2)}) collective-permute-start(bf16[4,272,128]{2,1,0:T(8,128)(2,1)S(1)} %shard_map.64.refs_5_.refs_8_), channel_id=1, source_target_pairs={{0,2},{2,0},{4,6},{6,4},{1,3},{3,1},{5,7},{7,5},{8,10},{10,8},{12,... | collective-permute-start | bytes 835592 | tf_op jit(solution)/shard_map/ppermute | solution.py:219
  10.9 8.9 %collective-permute-start = (bf16[4,272,128]{2,1,0:T(8,128)(2,1)S(1)}, bf16[4,272,128]{2,1,0:T(8,128)(2,1)S(1)}, u32[]{:S(2)}, u32[]{:S(2)}) collective-permute-start(bf16[4,272,128]{2,1,0:T(8,128)(2,1)S(1)} %shard_map.64.refs_5_.refs_8_), channel_id=1, source_target_pairs={{2,4},{4,2},{3,5},{5,3},{10,12},{12,10},{11,13},{13,11},{18,20},{2... | collective-permute-start | bytes 835592 | tf_op jit(solution)/shard_map/ppermute | solution.py:218
  13.6 15.6 %collective-permute-start.9 = (bf16[4,272,128]{2,1,0:T(8,128)(2,1)S(1)}, bf16[4,272,128]{2,1,0:T(8,128)(2,1)S(1)}, u32[]{:S(2)}, u32[]{:S(2)}) collective-permute-start(bf16[4,272,128]{2,1,0:T(8,128)(2,1)S(1)} %get-tuple-element.19.refs_5_.refs_8_.refs_10_), channel_id=1, source_target_pairs={{0,2},{2,0},{4,6},{6,4},{1,3},{3,1},{5,7},{7,5},{8,10},{10,8},{12,... | collective-permute-start | bytes 835592 | tf_op jit(solution)/shard_map/ppermute | solution.py:219
  19.1 10.7 %collective-permute-start.8 = (bf16[4,272,128]{2,1,0:T(8,128)(2,1)S(1)}, bf16[4,272,128]{2,1,0:T(8,128)(2,1)S(1)}, u32[]{:S(2)}, u32[]{:S(2)}) collective-permute-start(bf16[4,272,128]{2,1,0:T(8,128)(2,1)S(1)} %get-tuple-element.19.refs_5_.refs_8_.refs_10_), channel_id=1, source_target_pairs={{2,4},{4,2},{3,5},{5,3},{10,12},{12,10},{11,13},{13,11},{18,20},{2... | collective-permute-start | bytes 835592 | tf_op jit(solution)/shard_map/ppermute | solution.py:218
  21.1 10.2 %collective-permute-start.7 = (bf16[4,224,128]{2,1,0:T(8,128)(2,1)S(1)}, bf16[4,224,128]{2,1,0:T(8,128)(2,1)S(1)}, u32[]{:S(2)}, u32[]{:S(2)}) collective-permute-start(bf16[4,224,128]{2,1,0:T(8,128)(2,1)S(1)} %get-tuple-element.18.refs_5_.refs_8_), channel_id=1, source_target_pairs={{0,2},{2,0},{4,6},{6,4},{1,3},{3,1},{5,7},{7,5},{8,10},{10,8},{12,... | collective-permute-start | bytes 688136 | tf_op jit(solution)/shard_map/ppermute | solution.py:219
  24.5 6.8 %collective-permute-start.6 = (bf16[4,224,128]{2,1,0:T(8,128)(2,1)S(1)}, bf16[4,224,128]{2,1,0:T(8,128)(2,1)S(1)}, u32[]{:S(2)}, u32[]{:S(2)}) collective-permute-start(bf16[4,224,128]{2,1,0:T(8,128)(2,1)S(1)} %get-tuple-element.18.refs_5_.refs_8_), channel_id=1, source_target_pairs={{2,4},{4,2},{3,5},{5,3},{10,12},{12,10},{11,13},{13,11},{18,20},{2... | collective-permute-start | bytes 688136 | tf_op jit(solution)/shard_map/ppermute | solution.py:218
  25.2 4.7 %copy-start.2 = (bf16[2,128,256]{2,1,0:T(8,128)(2,1)S(1)}, bf16[2,128,256]{2,1,0:T(8,128)(2,1)}, u32[]{:S(2)}) copy-start(bf16[2,128,256]{2,1,0:T(8,128)(2,1)} %refs_3_.13) | copy-start | bytes 393220
  25.8 6.8 %collective-permute-start.5 = (bf16[4,80,128]{2,1,0:T(8,128)(2,1)S(1)}, bf16[4,80,128]{2,1,0:T(8,128)(2,1)S(1)}, u32[]{:S(2)}, u32[]{:S(2)}) collective-permute-start(bf16[4,80,128]{2,1,0:T(8,128)(2,1)S(1)} %shard_map.67.refs_5_), channel_id=1, source_target_pairs={{0,2},{2,0},{4,6},{6,4},{1,3},{3,1},{5,7},{7,5},{8,10},{10,8},{12,... | collective-permute-start | bytes 245768 | tf_op jit(solution)/shard_map/ppermute | solution.py:219
  29.1 3.5 %collective-permute-start.4 = (bf16[4,80,128]{2,1,0:T(8,128)(2,1)S(1)}, bf16[4,80,128]{2,1,0:T(8,128)(2,1)S(1)}, u32[]{:S(2)}, u32[]{:S(2)}) collective-permute-start(bf16[4,80,128]{2,1,0:T(8,128)(2,1)S(1)} %shard_map.67.refs_5_), channel_id=1, source_target_pairs={{2,4},{4,2},{3,5},{5,3},{10,12},{12,10},{11,13},{13,11},{18,20},{2... | collective-permute-start | bytes 245768 | tf_op jit(solution)/shard_map/ppermute | solution.py:218
